TPU v7x, 128 devices: a whole 4x4x4 slice. The times are simulated.
128 devices in a mesh: replica: 16 (over y, z), tensor: 8 (over x, core).
Axes of the slice: x: 4, y: 4, z: 4, core: 2. Of those that a mesh axis runs over, the one named last changes fastest.
Arguments:
- inner_change: bfloat16 [32768, 14336], P('replica', 'tensor'), may hold values from -6 to 6
- error_memory: bfloat16 [32768, 14336], P('replica', 'tensor'), may hold values from -4 to 4
- momentum: float32 [4096, 14336], P('replica', 'tensor'), may hold values from -2 to 2
- q_prev: float32 [32, 14336], P(None, 'tensor'), may hold values from -6 to 6
Outputs:
- outer_update: bfloat16 [4096, 14336], P('replica', 'tensor')
- new_momentum: float32 [4096, 14336], P('replica', 'tensor')
- new_error: bfloat16 [32768, 14336], P('replica', 'tensor')
- new_q: float32 [32, 14336], P(None, 'tensor')
All inputs are finite; a program needn't handle non-finite values.
Results may differ from a plain program's by a relative error of at most 0.003.
Values sent between devices are 32-bit elements; how exact they have to be, the bound alone decides.
No kernel may reach another device: no remote copies, remote signals or barrier semaphores. Data moves between devices by JAX's collectives and lax.ppermute only.
A program may use at most 128 MiB of HBM per device.

v0:
```python
import jax
import jax.numpy as jnp
from jax import lax
from jax.sharding import PartitionSpec as P


def orthonormal(summed):
    high = lax.Precision.HIGHEST
    gram_matrix = jnp.dot(summed, summed.T, precision=high, preferred_element_type=jnp.float32)
    factor = jnp.linalg.cholesky(gram_matrix)
    return jax.scipy.linalg.solve_triangular(factor, summed, lower=True)


def shards(inner_change, error_memory, momentum, q_prev):
    high = lax.Precision.HIGHEST
    combined = error_memory.astype(jnp.float32) - inner_change.astype(jnp.float32)
    half_rows = combined.shape[0]
    full_rows = 2 * half_rows
    rank_count = q_prev.shape[0]
    position = lax.axis_index("replica")
    start = position % 2 * half_rows
    partial_value = jnp.einsum(
        "cn,mn->cm", q_prev, combined, precision=high, preferred_element_type=jnp.float32
    )
    padded_term = lax.dynamic_update_slice(
        jnp.zeros((rank_count, full_rows), jnp.float32), partial_value, (jnp.int32(0), start)
    )
    summed = lax.psum(padded_term, ("replica", "tensor"))
    basis = orthonormal(summed)
    my_basis = lax.dynamic_slice_in_dim(basis, start, half_rows, 1)
    replica_count = lax.axis_size("replica") // 2
    projected = jnp.dot(my_basis, combined, precision=high, preferred_element_type=jnp.float32)
    coeffs = lax.psum(projected, "replica") / replica_count
    approx_mine = jnp.dot(my_basis.T, coeffs, precision=high, preferred_element_type=jnp.float32)
    new_error = (combined - approx_mine).astype(jnp.bfloat16)
    state_rows = momentum.shape[0]
    state_basis = lax.dynamic_slice_in_dim(basis, position * state_rows, state_rows, 1)
    approx_state = jnp.dot(
        state_basis.T, coeffs, precision=high, preferred_element_type=jnp.float32
    )
    new_momentum = 0.9 * momentum + approx_state
    outer_update = (0.7 * (approx_state + 0.9 * new_momentum)).astype(jnp.bfloat16)
    return (outer_update, new_momentum, new_error, coeffs)


def solution(mesh):
    in_specs = (
        P("replica", "tensor"),
        P("replica", "tensor"),
        P("replica", "tensor"),
        P(None, "tensor"),
    )
    out_specs = (
        P("replica", "tensor"),
        P("replica", "tensor"),
        P("replica", "tensor"),
        P(None, "tensor"),
    )
    return jax.shard_map(shards, mesh=mesh, in_specs=in_specs, out_specs=out_specs, check_vma=False)
```

profile of v0, /device:TPU:0, one launch (start us, length us, event | category | flops | bytes accessed | tf_op | source)
XLA Modules:
  0.0 309.5 jit_solution(9515534386390922396)
XLA Ops:
  7.2 0.0 copy-start
  7.2 0.0 all-reduce.3.cloned.1.call-start
  7.3 0.8 copy-done
  8.1 18.0 %fusion.3 = f32[32,4096]{1,0:T(8,128)S(1)} fusion(f32[32,4096]{1,0:T(8,128)S(1)} %broadcast_in_dim.5, s32[]{:T(128)S(6)} %select_n.19, f32[32,1792]{1,0:T(8,128)S(1)} %copy-done, bf16[2048,1792]{1,0:T(8,128)(2,1)} %param.4, bf16[2048,1792]{1,0:T(8,128)(2,1)} %param.5), kind=kOutput, calls=%fused_computation.5 | convolution fusion | flops 1420296192 | bytes 15171588 | tf_op jit(solution)/shard_map/cn,mn->cm/dot_general | solution.py:22
  26.1 0.0 copy-start.1
  26.1 0.8 copy-done.1
  26.9 0.0 all-reduce.3.cloned.1.call-update
  27.0 0.2 all-reduce.5.cloned.1.call-start
  27.2 147.0 %all-reduce.3.cloned.1.call-done = f32[32,4096]{1,0:T(8,128)} async-done(((f32[32,4096]{1,0:T(8,128)}), f32[32,4096]{1,0:T(8,128)}) %all-reduce.3.cloned.1.call-update) | async-done | bytes 524304 | tf_op jit(solution)/shard_map/psum | solution.py:28
  174.2 1.8 fusion.15
  176.0 0.1 copy.8
  176.1 2.9 cholesky.16
  179.0 0.6 compare_reduce_fusion
  179.7 0.7 fusion.8
  180.3 2.4 custom-call.7
  182.8 1.7 fusion.9
  184.5 13.3 %fusion = f32[32,1792]{1,0:T(8,128)} fusion(bf16[2048,1792]{1,0:T(8,128)(2,1)} %param.4, bf16[2048,1792]{1,0:T(8,128)(2,1)} %param.5, f32[32,4096]{1,0:T(8,128)S(1)} %fusion.9, s32[]{:T(128)S(6)} %select_n.19), kind=kOutput, calls=%fused_computation.2 | convolution fusion | flops 1420296192 | bytes 15171588 | tf_op jit(solution)/shard_map/dot_general | solution.py:32
  197.8 0.0 all-reduce.5.cloned.1.call-update
  197.8 83.8 %all-reduce.5.cloned.1.call-done = f32[32,1792]{1,0:T(8,128)} async-done(((f32[32,1792]{1,0:T(8,128)}), f32[32,1792]{1,0:T(8,128)}) %all-reduce.5.cloned.1.call-update) | async-done | bytes 229392 | tf_op jit(solution)/shard_map/psum | solution.py:33
  281.6 1.0 broadcast_multiply_fusion
  282.5 0.0 copy-start.2
  282.6 0.0 copy-start.3
  282.6 16.8 %subtract_convert_fusion = bf16[2048,1792]{1,0:T(8,128)(2,1)} fusion(bf16[2048,1792]{1,0:T(8,128)(2,1)} %param.4, bf16[2048,1792]{1,0:T(8,128)(2,1)} %param.5, f32[32,1792]{1,0:T(8,128)S(1)} %broadcast_multiply_fusion, f32[32,4096]{1,0:T(8,128)S(1)} %fusion.9, s32[]{:T(128)S(6)} %select_n.19), kind=kOutput, calls=%fused_computation | convolution fusion | flops 1427636224 | bytes 22511620 | tf_op jit(solution)/shard_map/dot_general | solution.py:34
  299.3 3.3 %multiply_convert_fusion = (bf16[256,1792]{1,0:T(8,128)(2,1)}, f32[256,1792]{1,0:T(8,128)}) fusion(f32[256,1792]{1,0:T(8,128)S(1)} %copy-done.3, f32[32,1792]{1,0:T(8,128)S(1)} %broadcast_multiply_fusion, f32[32,4096]{1,0:T(8,128)S(1)} %fusion.9, s32[]{:T(128)S(6)} %select_n.21), kind=kOutput, calls=%fused_computation.6 | convolution fusion | flops 178913280 | bytes 4849668 | tf_op jit(solution)/shard_map/dot_general | solution.py:38
  (5 shorter events, 0.1 us)
Async XLA Ops:
  7.2 0.9 copy-start
  7.2 167.0 %all-reduce.3.cloned.1.call-start = ((), (), s32[]{:S(2)}) async-start(), calls=%async_computation | async-start | bytes 1048576 | tf_op jit(solution)/shard_map/psum | solution.py:28
  26.1 0.8 copy-start.1
  27.0 254.6 %all-reduce.5.cloned.1.call-start = ((), (), s32[]{:S(2)}) async-start(), calls=%async_computation.1 | async-start | bytes 458752 | tf_op jit(solution)/shard_map/psum | solution.py:33
  282.5 16.8 %copy-start.2 = (f32[32,1792]{1,0:T(8,128)}, f32[32,1792]{1,0:T(8,128)S(1)}, u32[]{:S(2)}) copy-start(f32[32,1792]{1,0:T(8,128)S(1)} %broadcast_multiply_fusion) | copy-start | bytes 688132
  282.6 16.8 %copy-start.3 = (f32[256,1792]{1,0:T(8,128)S(1)}, f32[256,1792]{1,0:T(8,128)}, u32[]{:S(2)}) copy-start(f32[256,1792]{1,0:T(8,128)} %param.6) | copy-start | bytes 5505028
Sparse Core Ops, SparseCore 0:
  27.1 147.1 all-reduce.2
  197.9 83.6 all-reduce.4
where the time goes:
time: 310 us; the launch traced here: 309 us
  waiting for transfers between devices  231 us (75%)
  matrix products  54.9 us (18%)
  between operations  14.1 us (5%)
  other arithmetic  7.64 us (2%)
    psum x1, waiting for transfers between devices, shards(): summed = lax.psum(padded_term, ('replica', 'tensor'))  147 us
    psum x1, waiting for transfers between devices, shards(): coeffs = lax.psum(projected, 'replica') / replica_count  83.8 us
    dot_general x1, matrix products, shards(): jnp.einsum('cn,mn->cm', q_prev, combined, precision=high, preferred_eleme...  18 us
    dot_general x1, matrix products, shards(): jnp.dot(my_basis.T, coeffs, precision=high, preferred_element_type=jnp.fl...  16.8 us
    dot_general x1, matrix products, shards(): jnp.dot(my_basis, combined, precision=high, preferred_element_type=jnp.fl...  13.3 us
  transfers between devices with their start and end apart: 2, of which 2 were waited for; matrix products, arithmetic and copies ran while one was open for 0% of the time, Pallas kernels for 0%

commit v1 on v0

v1 whole, which is shorter than its diff:
```python
import jax
import jax.numpy as jnp
from jax import lax
from jax.experimental import pallas as pl
from jax.experimental.pallas import tpu as pltpu
from jax.sharding import PartitionSpec as P

RING = 4
BOTH = ("replica", "tensor")
RANK = 32
CHUNK = 256
STATE = 256
HBM = pl.BlockSpec(memory_space=pltpu.HBM)
VMEM = pl.BlockSpec(memory_space=pltpu.VMEM)


def swap_pairs(even, odd):
    pairs = []
    for device in range(RING**3 * 2):
        place = {
            "c": device % 2,
            "x": device // 2 % RING,
            "z": device // (2 * RING) % RING,
            "y": device // (2 * RING * RING),
        }
        axis, flip = (even, odd)[place["c"]]
        place[axis] ^= flip
        target = ((place["y"] * RING + place["z"]) * RING + place["x"]) * 2 + place["c"]
        pairs.append((device, target))
    return pairs


def swap(value, even, odd=None):
    return lax.ppermute(value, BOTH, swap_pairs(even, odd or even))


def sum_four(value, even, odd):
    one, two, three = (swap(value, (even, k), (odd, k)) for k in (1, 2, 3))
    return (value + one) + (two + three)


def split(value, count):
    parts = []
    for _ in range(count):
        part = value.astype(jnp.bfloat16)
        parts.append(part)
        value = value - part.astype(jnp.float32)
    return parts


def fold(value):
    return (value[:RANK] + value[RANK : 2 * RANK]) + value[2 * RANK : 3 * RANK]


NT = (((1,), (1,)), ((), ()))


def params(mebibytes):
    return pltpu.CompilerParams(vmem_limit_bytes=mebibytes * 1024 * 1024)


def core_of():
    return lax.rem(lax.axis_index("tensor"), 2)


def left_kernel(q_ref, error_hbm, change_hbm, send_ref, keep_ref, error_ref, change_ref, factor_ref, sems):
    core = core_of()
    half = send_ref.shape[1]
    count = 2 * half // CHUNK
    blocks, copies = [], []
    for k in range(count):
        side = (1 - core) if k < count // 2 else core
        rows = pl.ds(pl.multiple_of(side * half + k % (count // 2) * CHUNK, CHUNK), CHUNK)
        pair = [
            pltpu.make_async_copy(source.at[rows], target.at[rows], sems.at[j, k])
            for j, (source, target) in enumerate(((error_hbm, error_ref), (change_hbm, change_ref)))
        ]
        for copy in pair:
            copy.start()
        blocks.append(rows)
        copies.append(pair)
    parts = [part.astype(jnp.float32) for part in split(q_ref[...], 3)]
    stacked = jnp.concatenate(parts + [jnp.zeros_like(parts[0])], axis=0)
    factor_ref[...] = stacked.T.astype(jnp.bfloat16)
    for k in range(count):
        for copy in copies[k]:
            copy.wait()
        term = jnp.dot(error_ref[blocks[k], :], factor_ref[...], preferred_element_type=jnp.float32)
        term -= jnp.dot(change_ref[blocks[k], :], factor_ref[...], preferred_element_type=jnp.float32)
        target = send_ref if k < count // 2 else keep_ref
        start = k % (count // 2) * CHUNK
        target[:, start : start + CHUNK] = fold(term.T)


def left_factor(q_prev, error_memory, inner_change):
    rows, columns = error_memory.shape
    half = rows // 2
    return pl.pallas_call(
        left_kernel,
        in_specs=[VMEM, HBM, HBM],
        out_specs=[VMEM] * 4,
        out_shape=[
            pltpu.VMEM((RANK, half), jnp.float32),
            pltpu.VMEM((RANK, half), jnp.float32),
            pltpu.VMEM((rows, columns), jnp.bfloat16),
            pltpu.VMEM((rows, columns), jnp.bfloat16),
        ],
        scratch_shapes=[
            pltpu.VMEM((columns, 4 * RANK), jnp.bfloat16),
            pltpu.SemaphoreType.DMA((2, rows // CHUNK)),
        ],
        compiler_params=params(8),
        cost_estimate=pl.CostEstimate(
            flops=12 * RANK * rows * columns, bytes_accessed=4 * rows * columns, transcendentals=0
        ),
        name="left_factor",
    )(q_prev, pltpu.with_memory_space_constraint(error_memory, pltpu.HBM),
      pltpu.with_memory_space_constraint(inner_change, pltpu.HBM))


def right_products(left_ref, error_ref, change_ref, side, previous_ref, out_ref):
    half, columns = left_ref.shape[1], error_ref.shape[1]
    rows = pl.ds(pl.multiple_of(side * half, half), half)
    factor = jnp.concatenate(split(left_ref[...], 3), axis=0)
    for start in range(0, columns, CHUNK):
        block = slice(start, start + CHUNK)
        term = jnp.dot(factor, error_ref[rows, block], preferred_element_type=jnp.float32)
        term -= jnp.dot(factor, change_ref[rows, block], preferred_element_type=jnp.float32)
        value = fold(term)
        if previous_ref is not None:
            value = value + previous_ref[:, block]
        out_ref[:, block] = value
    squares = fold(lax.dot_general(factor, factor, NT, preferred_element_type=jnp.float32))
    return (squares[:, :RANK] + squares[:, RANK : 2 * RANK]) + squares[:, 2 * RANK :]


def first_kernel(own_ref, error_ref, change_ref, out_ref, gram_ref):
    gram = right_products(own_ref, error_ref, change_ref, core_of(), None, out_ref)
    gram_ref[...] = jnp.concatenate([gram, jnp.zeros((RANK, 128 - RANK), jnp.float32)], axis=1)


def second_kernel(own_ref, other_ref, error_ref, change_ref, previous_ref, gram_ref, out_ref, whole_ref, share_ref):
    core = core_of()
    half = own_ref.shape[1]
    gram = right_products(other_ref, error_ref, change_ref, 1 - core, previous_ref, out_ref)
    share_ref[:, :128] = gram_ref[...] + jnp.concatenate(
        [gram, jnp.zeros((RANK, 128 - RANK), jnp.float32)], axis=1
    )
    whole_ref[:, pl.ds(pl.multiple_of(core * half, half), half)] = own_ref[...]
    whole_ref[:, pl.ds(pl.multiple_of((1 - core) * half, half), half)] = other_ref[...]
    position = lax.axis_index("replica")
    neighbour = position + 1 - 2 * lax.rem(position, 2)
    start = lax.rem(neighbour, 8) * STATE
    share_ref[:, 128:] = whole_ref[:, pl.ds(pl.multiple_of(start, STATE), STATE)]


def right_factor(own, other, error, change):
    rows, columns = error.shape
    half = own.shape[1]
    cost = pl.CostEstimate(
        flops=12 * RANK * half * columns, bytes_accessed=4 * half * columns, transcendentals=0
    )
    projected, gram = pl.pallas_call(
        first_kernel,
        in_specs=[VMEM] * 3,
        out_specs=[VMEM] * 2,
        out_shape=[
            pltpu.VMEM((RANK, columns), jnp.float32),
            pltpu.VMEM((RANK, 128), jnp.float32),
        ],
        compiler_params=params(8),
        cost_estimate=cost,
        name="right_first",
    )(own, error, change)
    return pl.pallas_call(
        second_kernel,
        in_specs=[VMEM] * 6,
        out_specs=[VMEM] * 3,
        out_shape=[
            pltpu.VMEM((RANK, columns), jnp.float32),
            pltpu.VMEM((RANK, rows), jnp.float32),
            pltpu.VMEM((RANK, 128 + STATE), jnp.float32),
        ],
        compiler_params=params(8),
        cost_estimate=cost,
        name="right_second",
    )(own, other, error, change, projected, gram)


def basis_kernel(whole_ref, mine_ref, theirs_ref, inverse_ref, basis_ref):
    width = 128
    row = lax.broadcasted_iota(jnp.int32, (RANK, width), 0)
    column = lax.broadcasted_iota(jnp.int32, (RANK, width), 1)
    gram = mine_ref[:, :width] + theirs_ref[:, :width]
    work = jnp.where(column < RANK, gram, jnp.where(column - RANK == row, 1.0, 0.0))
    for j in range(RANK):
        pivot = work[j : j + 1, :]
        scale = lax.rsqrt(pivot[:, j : j + 1])
        scaled = pivot * scale
        factor = work[:, j : j + 1] * scale
        work = jnp.where(row > j, work - factor * scaled, jnp.where(row == j, scaled, work))
    inverse = work[:, RANK : 2 * RANK]
    inverse_ref[...] = jnp.concatenate([inverse, jnp.zeros((RANK, width - RANK), jnp.float32)], axis=1)
    rows = whole_ref.shape[1]
    position = lax.axis_index("replica")
    start = lax.rem(position, 8) * STATE
    mine = whole_ref[:, pl.ds(pl.multiple_of(start, STATE), STATE)]
    state = jnp.where(lax.rem(position, 2) == position // 8, mine, theirs_ref[:, width:])
    for offset, count, value in ((0, rows, whole_ref[...]), (rows, STATE, state)):
        basis = jnp.dot(inverse, value, precision=lax.Precision.HIGHEST, preferred_element_type=jnp.float32)
        top, low = (part.astype(jnp.float32) for part in split(basis, 2))
        stacked = jnp.concatenate([top, low, top, low], axis=0)
        basis_ref[offset : offset + count, :] = stacked.T.astype(jnp.bfloat16)


def make_basis(whole, mine, theirs):
    rows = whole.shape[1]
    return pl.pallas_call(
        basis_kernel,
        in_specs=[VMEM] * 3,
        out_specs=[VMEM, VMEM],
        out_shape=[
            pltpu.VMEM((RANK, 128), jnp.float32),
            pltpu.VMEM((rows + STATE, 128), jnp.bfloat16),
        ],
        compiler_params=params(8),
        cost_estimate=pl.CostEstimate(
            flops=24 * RANK * RANK * rows, bytes_accessed=16 * RANK * rows, transcendentals=0
        ),
        name="basis",
    )(whole, mine, theirs)


def apply_kernel(
    count, summed_ref, inverse_ref, basis_ref, error_ref, change_ref, momentum_ref,
    update_hbm, momentum_hbm, error_hbm, q_ref,
    momentum_out_ref, update_ref, error_out_ref, sems,
):
    rows, columns = error_ref.shape
    new_q = (
        jnp.dot(
            inverse_ref[:, :RANK], summed_ref[...],
            precision=lax.Precision.HIGHEST, preferred_element_type=jnp.float32,
        )
        / count
    )
    q_ref[...] = new_q
    top, low = split(new_q, 2)
    factor = jnp.concatenate([top, top, low, low], axis=0)
    started = []
    for k in range(rows // CHUNK):
        block = pl.ds(k * CHUNK, CHUNK)
        approx = jnp.dot(basis_ref[block, :], factor, preferred_element_type=jnp.float32)
        combined = error_ref[block, :].astype(jnp.float32) - change_ref[block, :].astype(jnp.float32)
        error_out_ref[block, :] = (combined - approx).astype(jnp.bfloat16)
        copy = pltpu.make_async_copy(error_out_ref.at[block], error_hbm.at[block], sems.at[2 + k])
        copy.start()
        started.append(copy)
    approx = jnp.dot(basis_ref[pl.ds(rows, STATE), :], factor, preferred_element_type=jnp.float32)
    momentum = 0.9 * momentum_ref[...] + approx
    momentum_out_ref[...] = momentum
    update_ref[...] = (0.7 * (approx + 0.9 * momentum)).astype(jnp.bfloat16)
    for copy in (
        pltpu.make_async_copy(momentum_out_ref, momentum_hbm, sems.at[0]),
        pltpu.make_async_copy(update_ref, update_hbm, sems.at[1]),
    ):
        copy.start()
        started.append(copy)
    for copy in started:
        copy.wait()


def apply_factors(count, summed, inverse, basis, error, change, momentum):
    rows, columns = error.shape
    state = momentum.shape
    return pl.pallas_call(
        lambda *refs: apply_kernel(count, *refs),
        in_specs=[VMEM] * 6,
        out_specs=[HBM, HBM, HBM, VMEM],
        out_shape=[
            pltpu.HBM(state, jnp.bfloat16),
            pltpu.HBM(state, jnp.float32),
            pltpu.HBM((rows, columns), jnp.bfloat16),
            jax.ShapeDtypeStruct((RANK, columns), jnp.float32),
        ],
        scratch_shapes=[
            pltpu.VMEM(state, jnp.float32),
            pltpu.VMEM(state, jnp.bfloat16),
            pltpu.VMEM((rows, columns), jnp.bfloat16),
            pltpu.SemaphoreType.DMA((2 + rows // CHUNK,)),
        ],
        compiler_params=params(18),
        cost_estimate=pl.CostEstimate(
            flops=8 * RANK * rows * columns, bytes_accessed=6 * rows * columns, transcendentals=0
        ),
        name="apply",
    )(summed, inverse, basis, error, change, momentum)


def shards(inner_change, error_memory, momentum, q_prev):
    replicas = lax.axis_size("replica") // 2

    send, keep, error, change = left_factor(q_prev, error_memory, inner_change)
    own = keep + swap(send, ("c", 1))
    own = sum_four(own, "x", "y")
    own = sum_four(own, "y", "x")
    own = own + swap(own, ("z", 2))
    other = swap(own, ("c", 1))

    projected, whole, mine = right_factor(own, other, error, change)
    theirs = swap(mine, ("z", 1))
    summed = sum_four(projected, "y", "z")
    summed, theirs = lax.optimization_barrier((summed, theirs))
    inverse, basis = make_basis(whole, mine, theirs)
    summed = sum_four(summed, "z", "y")
    update, new_momentum, new_error, new_q = apply_factors(
        replicas, summed, inverse, basis, error, change, momentum
    )
    return (update, new_momentum, new_error, new_q)


def solution(mesh):
    in_specs = (
        P("replica", "tensor"),
        P("replica", "tensor"),
        P("replica", "tensor"),
        P(None, "tensor"),
    )
    out_specs = (
        P("replica", "tensor"),
        P("replica", "tensor"),
        P("replica", "tensor"),
        P(None, "tensor"),
    )
    return jax.shard_map(shards, mesh=mesh, in_specs=in_specs, out_specs=out_specs, check_vma=False)
```

time: 310 us -> 66.8 us (0.22)
  waiting for transfers between devices: 231 us -> 23.3 us
  matrix products: 54.9 us -> 0 us
  starting transfers between devices: 0.26 us -> 22.9 us
  Pallas kernels: 0 us -> 18.4 us
  between operations: 14.1 us -> 0.9 us
  other arithmetic: 7.64 us -> 0.18 us
    psum x2 -> x0, waiting for transfers between devices: 231 us -> none  [the longest x1 147 us: shards(): summed = lax.psum(padded_term, ('replica', 'tensor'))]
    dot_general x5 -> x0, matrix products: 53.2 us -> none  [the longest x1 18 us: shards(): jnp.einsum('cn,mn->cm', q_prev, combined, precision=high, preferred_eleme...]
    ppermute x0 -> x16, waiting for transfers between devices: none -> 23.3 us  [swap(): return lax.ppermute(value, BOTH, swap_pairs(even, odd or even))]
    ppermute x0 -> x16, starting transfers between devices: none -> 22.9 us  [swap(): return lax.ppermute(value, BOTH, swap_pairs(even, odd or even))]
    pallas_call x0 -> x5, Pallas kernels: none -> 18.4 us  [the longest x1 7.24 us: left_factor(): pl.pallas_call(left_kernel, in_specs=[VMEM, HBM, HBM], out_specs=[VMEM] *...]
    another operation x5 -> x0, other arithmetic: 6.68 us -> none  [the longest x3 3.6 us: orthonormal(): factor = jnp.linalg.cholesky(gram_matrix)]
  transfers between devices with their start and end apart: 2 -> 16, of which waited for: 2 -> 10; matrix products, arithmetic and copies ran while one was open for 0% -> 0% of each run, Pallas kernels for 0% -> 7%
where the time goes in v1:
time: 66.8 us; the launch traced here: 66.6 us
  waiting for transfers between devices  23.3 us (35%)
  starting transfers between devices  22.9 us (34%)
  Pallas kernels  18.4 us (28%)
  local copies, waits for them, and re-layouts  0.94 us (1%)
  between operations  0.9 us (1%)
    ppermute x16, waiting for transfers between devices, swap(): return lax.ppermute(value, BOTH, swap_pairs(even, odd or even))  23.3 us
    ppermute x16, starting transfers between devices, swap(): return lax.ppermute(value, BOTH, swap_pairs(even, odd or even))  22.9 us
    pallas_call x1, Pallas kernels, left_factor(): pl.pallas_call(left_kernel, in_specs=[VMEM, HBM, HBM], out_specs=[VMEM] *...  7.24 us
    pallas_call x1, Pallas kernels, apply_factors(): pl.pallas_call(lambda *refs: apply_kernel(count, *refs), in_specs=[VMEM]...  5.19 us
    pallas_call x1, Pallas kernels, make_basis(): pl.pallas_call(basis_kernel, in_specs=[VMEM] * 3, out_specs=[VMEM, VMEM],...  3.13 us
    pallas_call x1, Pallas kernels, right_factor(): pl.pallas_call(second_kernel, in_specs=[VMEM] * 6, out_specs=[VMEM] * 3,...  1.43 us
    pallas_call x1, Pallas kernels, right_factor(): pl.pallas_call(first_kernel, in_specs=[VMEM] * 3, out_specs=[VMEM] * 2, o...  1.42 us
  transfers between devices with their start and end apart: 16, of which 10 were waited for; matrix products, arithmetic and copies ran while one was open for 0% of the time, Pallas kernels for 7%

profile of v1, /device:TPU:0, one launch (start us, length us, event | category | flops | bytes accessed | tf_op | source)
XLA Modules:
  0.0 66.6 jit_solution(16653430359373101708)
XLA Ops:
  0.6 0.9 %copy-done.1 = f32[32,1792]{1,0:T(8,128)S(1)} copy-done((f32[32,1792]{1,0:T(8,128)S(1)}, f32[32,1792]{1,0:T(8,128)}, u32[]{:S(2)}) %copy-start.1) | copy-done | bytes 229400
  1.6 7.2 %left_factor.1 = (f32[32,1024]{1,0:T(8,128)S(1)}, f32[32,1024]{1,0:T(8,128)S(1)}, bf16[2048,1792]{1,0:T(8,128)(2,1)S(1)}, bf16[2048,1792]{1,0:T(8,128)(2,1)S(1)}) custom-call(f32[32,1792]{1,0:T(8,128)S(1)} %copy-done.1, bf16[2048,1792]{1,0:T(8,128)(2,1)} %error_hbm.1, bf16[2048,1792]{1,0:T(8,128)(2,1)} %change_hbm.1), custom_call_target="tpu_custom_call" | custom-call | flops 1409286144 | bytes 14680064 | tf_op jit(solution)/shard_map/left_factor/pallas_call | solution.py:98
  8.9 1.3 %collective-permute-done = f32[32,1024]{1,0:T(8,128)S(1)} collective-permute-done((f32[32,1024]{1,0:T(8,128)S(1)}, f32[32,1024]{1,0:T(8,128)S(1)}, u32[]{:S(2)}, u32[]{:S(2)}) %collective-permute-start) | collective-permute-done | bytes 131104 | tf_op jit(solution)/shard_map/ppermute | solution.py:34
  10.3 2.9 %collective-permute-start.3 = (f32[32,1024]{1,0:T(8,128)S(1)}, f32[32,1024]{1,0:T(8,128)S(1)}, u32[]{:S(2)}, u32[]{:S(2)}) collective-permute-start(f32[32,1024]{1,0:T(8,128)S(1)} %add.42), channel_id=1, source_target_pairs={{0,6},{1,97},{2,4},{3,99},{4,2},{5,101},{6,0},{7,103},{8,14},{9,10... | collective-permute-start | bytes 393224 | tf_op jit(solution)/shard_map/ppermute | solution.py:34
  14.4 2.7 %collective-permute-done.3 = f32[32,1024]{1,0:T(8,128)S(1)} collective-permute-done((f32[32,1024]{1,0:T(8,128)S(1)}, f32[32,1024]{1,0:T(8,128)S(1)}, u32[]{:S(2)}, u32[]{:S(2)}) %collective-permute-start.3) | collective-permute-done | bytes 131104 | tf_op jit(solution)/shard_map/ppermute | solution.py:34
  17.1 2.5 %collective-permute-done.2 = f32[32,1024]{1,0:T(8,128)S(1)} collective-permute-done((f32[32,1024]{1,0:T(8,128)S(1)}, f32[32,1024]{1,0:T(8,128)S(1)}, u32[]{:S(2)}, u32[]{:S(2)}) %collective-permute-start.2) | collective-permute-done | bytes 131104 | tf_op jit(solution)/shard_map/ppermute | solution.py:34
  19.7 3.1 %collective-permute-start.6 = (f32[32,1024]{1,0:T(8,128)S(1)}, f32[32,1024]{1,0:T(8,128)S(1)}, u32[]{:S(2)}, u32[]{:S(2)}) collective-permute-start(f32[32,1024]{1,0:T(8,128)S(1)} %add_add_fusion.3), channel_id=1, source_target_pairs={{0,96},{1,7},{2,98},{3,5},{4,100},{5,3},{6,102},{7,1},{8,104},{9,1... | collective-permute-start | bytes 393224 | tf_op jit(solution)/shard_map/ppermute | solution.py:34
  23.9 2.8 %collective-permute-done.6 = f32[32,1024]{1,0:T(8,128)S(1)} collective-permute-done((f32[32,1024]{1,0:T(8,128)S(1)}, f32[32,1024]{1,0:T(8,128)S(1)}, u32[]{:S(2)}, u32[]{:S(2)}) %collective-permute-start.6) | collective-permute-done | bytes 131104 | tf_op jit(solution)/shard_map/ppermute | solution.py:34
  26.7 2.5 %collective-permute-done.5 = f32[32,1024]{1,0:T(8,128)S(1)} collective-permute-done((f32[32,1024]{1,0:T(8,128)S(1)}, f32[32,1024]{1,0:T(8,128)S(1)}, u32[]{:S(2)}, u32[]{:S(2)}) %collective-permute-start.5) | collective-permute-done | bytes 131104 | tf_op jit(solution)/shard_map/ppermute | solution.py:34
  29.3 4.0 %collective-permute-start.7 = (f32[32,1024]{1,0:T(8,128)S(1)}, f32[32,1024]{1,0:T(8,128)S(1)}, u32[]{:S(2)}, u32[]{:S(2)}) collective-permute-start(f32[32,1024]{1,0:T(8,128)S(1)} %add_add_fusion.2), channel_id=1, source_target_pairs={{0,16},{1,17},{2,18},{3,19},{4,20},{5,21},{6,22},{7,23},{8,24},{9,... | collective-permute-start | bytes 393224 | tf_op jit(solution)/shard_map/ppermute | solution.py:34
  33.3 2.9 %collective-permute-done.7 = f32[32,1024]{1,0:T(8,128)S(1)} collective-permute-done((f32[32,1024]{1,0:T(8,128)S(1)}, f32[32,1024]{1,0:T(8,128)S(1)}, u32[]{:S(2)}, u32[]{:S(2)}) %collective-permute-start.7) | collective-permute-done | bytes 131104 | tf_op jit(solution)/shard_map/ppermute | solution.py:34
  36.3 1.4 %right_first.1 = (f32[32,1792]{1,0:T(8,128)S(1)}, f32[32,128]{1,0:T(8,128)S(1)}) custom-call(f32[32,1024]{1,0:T(8,128)S(1)} %add.49.own_ref, bf16[2048,1792]{1,0:T(8,128)(2,1)S(1)} %get-tuple-element.19.error_ref.refs_3_, bf16[2048,1792]{1,0:T(8,128)(2,1)S(1)} %get-tuple-element.20.change_ref.refs_4_), custom_call_target="tpu_custom_call" | custom-call | flops 704643072 | bytes 7340032 | tf_op jit(solution)/shard_map/right_first/pallas_call | solution.py:163
  37.8 1.4 %right_second.1 = (f32[32,1792]{1,0:T(8,128)S(1)}, f32[32,2048]{1,0:T(8,128)S(1)}, f32[32,384]{1,0:T(8,128)S(1)}) custom-call(f32[32,1024]{1,0:T(8,128)S(1)} %add.49.own_ref, f32[32,1024]{1,0:T(8,128)S(1)} %collective-permute-done.8.other_ref, bf16[2048,1792]{1,0:T(8,128)(2,1)S(1)} %get-tuple-element.19.error_ref.refs_3_, ...), custom_call_target="tpu_custom_call" | custom-call | flops 704643072 | bytes 7340032 | tf_op jit(solution)/shard_map/right_second/pallas_call | solution.py:175
  39.2 2.0 %collective-permute-start.11 = (f32[32,1792]{1,0:T(8,128)S(1)}, f32[32,1792]{1,0:T(8,128)S(1)}, u32[]{:S(2)}, u32[]{:S(2)}) collective-permute-start(f32[32,1792]{1,0:T(8,128)S(1)} %get-tuple-element.23), channel_id=1, source_target_pairs={{0,96},{1,25},{2,98},{3,27},{4,100},{5,29},{6,102},{7,31},{8,104},... | collective-permute-start | bytes 688136 | tf_op jit(solution)/shard_map/ppermute | solution.py:34
  41.9 1.5 %collective-permute-start.9 = (f32[32,1792]{1,0:T(8,128)S(1)}, f32[32,1792]{1,0:T(8,128)S(1)}, u32[]{:S(2)}, u32[]{:S(2)}) collective-permute-start(f32[32,1792]{1,0:T(8,128)S(1)} %get-tuple-element.23), channel_id=1, source_target_pairs={{0,32},{1,9},{2,34},{3,11},{4,36},{5,13},{6,38},{7,15},{8,40},{9,1... | collective-permute-start | bytes 688136 | tf_op jit(solution)/shard_map/ppermute | solution.py:34
  43.4 1.6 %collective-permute-start.12 = (f32[32,384]{1,0:T(8,128)S(1)}, f32[32,384]{1,0:T(8,128)S(1)}, u32[]{:S(2)}, u32[]{:S(2)}) collective-permute-start(f32[32,384]{1,0:T(8,128)S(1)} %get-tuple-element.24.mine_ref), channel_id=1, source_target_pairs={{0,8},{1,9},{2,10},{3,11},{4,12},{5,13},{6,14},{7,15},{8,0},{9,1},... | collective-permute-start | bytes 147464 | tf_op jit(solution)/shard_map/ppermute | solution.py:34
  44.9 4.0 %collective-permute-done.11 = f32[32,1792]{1,0:T(8,128)S(1)} collective-permute-done((f32[32,1792]{1,0:T(8,128)S(1)}, f32[32,1792]{1,0:T(8,128)S(1)}, u32[]{:S(2)}, u32[]{:S(2)}) %collective-permute-start.11) | collective-permute-done | bytes 229408 | tf_op jit(solution)/shard_map/ppermute | solution.py:34
  49.0 0.9 %collective-permute-done.9 = f32[32,1792]{1,0:T(8,128)S(1)} collective-permute-done((f32[32,1792]{1,0:T(8,128)S(1)}, f32[32,1792]{1,0:T(8,128)S(1)}, u32[]{:S(2)}, u32[]{:S(2)}) %collective-permute-start.9) | collective-permute-done | bytes 229408 | tf_op jit(solution)/shard_map/ppermute | solution.py:34
  49.9 3.8 %collective-permute-start.15 = (f32[32,1792]{1,0:T(8,128)S(1)}, f32[32,1792]{1,0:T(8,128)S(1)}, u32[]{:S(2)}, u32[]{:S(2)}) collective-permute-start(f32[32,1792]{1,0:T(8,128)S(1)} %add_add_fusion.1), channel_id=1, source_target_pairs={{0,24},{1,97},{2,26},{3,99},{4,28},{5,101},{6,30},{7,103},{8,16},{... | collective-permute-start | bytes 688136 | tf_op jit(solution)/shard_map/ppermute | solution.py:34
  53.7 0.9 %collective-permute-start.13 = (f32[32,1792]{1,0:T(8,128)S(1)}, f32[32,1792]{1,0:T(8,128)S(1)}, u32[]{:S(2)}, u32[]{:S(2)}) collective-permute-start(f32[32,1792]{1,0:T(8,128)S(1)} %add_add_fusion.1), channel_id=1, source_target_pairs={{0,8},{1,33},{2,10},{3,35},{4,12},{5,37},{6,14},{7,39},{8,0},{9,41... | collective-permute-start | bytes 688136 | tf_op jit(solution)/shard_map/ppermute | solution.py:34
  54.6 3.1 %basis.1 = (f32[32,128]{1,0:T(8,128)S(1)}, bf16[2304,128]{1,0:T(8,128)(2,1)S(1)}) custom-call(f32[32,2048]{1,0:T(8,128)S(1)} %get-tuple-element.26.whole_ref, f32[32,384]{1,0:T(8,128)S(1)} %get-tuple-element.24.mine_ref, f32[32,384]{1,0:T(8,128)S(1)} %collective-permute-done.12.theirs_ref), custom_call_target="tpu_custom_call" | custom-call | flops 50331648 | bytes 1048576 | tf_op jit(solution)/shard_map/basis/pallas_call | solution.py:218
  57.8 1.9 %collective-permute-done.15 = f32[32,1792]{1,0:T(8,128)S(1)} collective-permute-done((f32[32,1792]{1,0:T(8,128)S(1)}, f32[32,1792]{1,0:T(8,128)S(1)}, u32[]{:S(2)}, u32[]{:S(2)}) %collective-permute-start.15) | collective-permute-done | bytes 229408 | tf_op jit(solution)/shard_map/ppermute | solution.py:34
  59.7 1.5 %collective-permute-done.14 = f32[32,1792]{1,0:T(8,128)S(1)} collective-permute-done((f32[32,1792]{1,0:T(8,128)S(1)}, f32[32,1792]{1,0:T(8,128)S(1)}, u32[]{:S(2)}, u32[]{:S(2)}) %collective-permute-start.14) | collective-permute-done | bytes 229408 | tf_op jit(solution)/shard_map/ppermute | solution.py:34
  61.3 5.2 %apply.1 = (bf16[256,1792]{1,0:T(8,128)(2,1)}, f32[256,1792]{1,0:T(8,128)}, bf16[2048,1792]{1,0:T(8,128)(2,1)}, f32[32,1792]{1,0:T(8,128)}) custom-call(f32[32,1792]{1,0:T(8,128)S(1)} %add_add_fusion.refs_0_, f32[32,128]{1,0:T(8,128)S(1)} %get-tuple-element.28.refs_1_, bf16[2304,128]{1,0:T(8,128)(2,1)S(1)} %get-tuple-element.29.refs_2_, ...), custom_call_target="tpu_custom_call" | custom-call | flops 939524096 | bytes 22020096 | tf_op jit(solution)/shard_map/apply/pallas_call | solution.py:276
  (23 shorter events, 3.3 us)
Async XLA Ops:
  0.6 0.9 %copy-start.1 = (f32[32,1792]{1,0:T(8,128)S(1)}, f32[32,1792]{1,0:T(8,128)}, u32[]{:S(2)}) copy-start(f32[32,1792]{1,0:T(8,128)} %q_ref.1) | copy-start | bytes 688132
  8.8 1.4 %collective-permute-start = (f32[32,1024]{1,0:T(8,128)S(1)}, f32[32,1024]{1,0:T(8,128)S(1)}, u32[]{:S(2)}, u32[]{:S(2)}) collective-permute-start(f32[32,1024]{1,0:T(8,128)S(1)} %get-tuple-element.18), channel_id=1, source_target_pairs={{0,1},{1,0},{2,3},{3,2},{4,5},{5,4},{6,7},{7,6},{8,9},{9,8},{10,11... | collective-permute-start | bytes 393224 | tf_op jit(solution)/shard_map/ppermute | solution.py:34
  10.3 6.8 %collective-permute-start.3 = (f32[32,1024]{1,0:T(8,128)S(1)}, f32[32,1024]{1,0:T(8,128)S(1)}, u32[]{:S(2)}, u32[]{:S(2)}) collective-permute-start(f32[32,1024]{1,0:T(8,128)S(1)} %add.42), channel_id=1, source_target_pairs={{0,6},{1,97},{2,4},{3,99},{4,2},{5,101},{6,0},{7,103},{8,14},{9,10... | collective-permute-start | bytes 393224 | tf_op jit(solution)/shard_map/ppermute | solution.py:34
  13.2 6.5 %collective-permute-start.2 = (f32[32,1024]{1,0:T(8,128)S(1)}, f32[32,1024]{1,0:T(8,128)S(1)}, u32[]{:S(2)}, u32[]{:S(2)}) collective-permute-start(f32[32,1024]{1,0:T(8,128)S(1)} %add.42), channel_id=1, source_target_pairs={{0,4},{1,65},{2,6},{3,67},{4,0},{5,69},{6,2},{7,71},{8,12},{9,73},... | collective-permute-start | bytes 393224 | tf_op jit(solution)/shard_map/ppermute | solution.py:34
  14.0 5.7 %collective-permute-start.1 = (f32[32,1024]{1,0:T(8,128)S(1)}, f32[32,1024]{1,0:T(8,128)S(1)}, u32[]{:S(2)}, u32[]{:S(2)}) collective-permute-start(f32[32,1024]{1,0:T(8,128)S(1)} %add.42), channel_id=1, source_target_pairs={{0,2},{1,33},{2,0},{3,35},{4,6},{5,37},{6,4},{7,39},{8,10},{9,41},... | collective-permute-start | bytes 393224 | tf_op jit(solution)/shard_map/ppermute | solution.py:34
  19.7 7.0 %collective-permute-start.6 = (f32[32,1024]{1,0:T(8,128)S(1)}, f32[32,1024]{1,0:T(8,128)S(1)}, u32[]{:S(2)}, u32[]{:S(2)}) collective-permute-start(f32[32,1024]{1,0:T(8,128)S(1)} %add_add_fusion.3), channel_id=1, source_target_pairs={{0,96},{1,7},{2,98},{3,5},{4,100},{5,3},{6,102},{7,1},{8,104},{9,1... | collective-permute-start | bytes 393224 | tf_op jit(solution)/shard_map/ppermute | solution.py:34
  22.8 6.5 %collective-permute-start.5 = (f32[32,1024]{1,0:T(8,128)S(1)}, f32[32,1024]{1,0:T(8,128)S(1)}, u32[]{:S(2)}, u32[]{:S(2)}) collective-permute-start(f32[32,1024]{1,0:T(8,128)S(1)} %add_add_fusion.3), channel_id=1, source_target_pairs={{0,64},{1,5},{2,66},{3,7},{4,68},{5,1},{6,70},{7,3},{8,72},{9,13},... | collective-permute-start | bytes 393224 | tf_op jit(solution)/shard_map/ppermute | solution.py:34
  23.4 5.8 %collective-permute-start.4 = (f32[32,1024]{1,0:T(8,128)S(1)}, f32[32,1024]{1,0:T(8,128)S(1)}, u32[]{:S(2)}, u32[]{:S(2)}) collective-permute-start(f32[32,1024]{1,0:T(8,128)S(1)} %add_add_fusion.3), channel_id=1, source_target_pairs={{0,32},{1,3},{2,34},{3,1},{4,36},{5,7},{6,38},{7,5},{8,40},{9,11},... | collective-permute-start | bytes 393224 | tf_op jit(solution)/shard_map/ppermute | solution.py:34
  29.3 6.9 %collective-permute-start.7 = (f32[32,1024]{1,0:T(8,128)S(1)}, f32[32,1024]{1,0:T(8,128)S(1)}, u32[]{:S(2)}, u32[]{:S(2)}) collective-permute-start(f32[32,1024]{1,0:T(8,128)S(1)} %add_add_fusion.2), channel_id=1, source_target_pairs={{0,16},{1,17},{2,18},{3,19},{4,20},{5,21},{6,22},{7,23},{8,24},{9,... | collective-permute-start | bytes 393224 | tf_op jit(solution)/shard_map/ppermute | solution.py:34
  36.2 1.5 %collective-permute-start.8 = (f32[32,1024]{1,0:T(8,128)S(1)}, f32[32,1024]{1,0:T(8,128)S(1)}, u32[]{:S(2)}, u32[]{:S(2)}) collective-permute-start(f32[32,1024]{1,0:T(8,128)S(1)} %add.49.own_ref), channel_id=1, source_target_pairs={{0,1},{1,0},{2,3},{3,2},{4,5},{5,4},{6,7},{7,6},{8,9},{9,8},{10,11... | collective-permute-start | bytes 393224 | tf_op jit(solution)/shard_map/ppermute | solution.py:34
  37.8 23.5 %copy-start = (f32[256,1792]{1,0:T(8,128)S(1)}, f32[256,1792]{1,0:T(8,128)}, u32[]{:S(2)}) copy-start(f32[256,1792]{1,0:T(8,128)} %refs_5_.1) | copy-start | bytes 5505028
  39.2 9.8 %collective-permute-start.11 = (f32[32,1792]{1,0:T(8,128)S(1)}, f32[32,1792]{1,0:T(8,128)S(1)}, u32[]{:S(2)}, u32[]{:S(2)}) collective-permute-start(f32[32,1792]{1,0:T(8,128)S(1)} %get-tuple-element.23), channel_id=1, source_target_pairs={{0,96},{1,25},{2,98},{3,27},{4,100},{5,29},{6,102},{7,31},{8,104},... | collective-permute-start | bytes 688136 | tf_op jit(solution)/shard_map/ppermute | solution.py:34
  41.2 7.7 %collective-permute-start.10 = (f32[32,1792]{1,0:T(8,128)S(1)}, f32[32,1792]{1,0:T(8,128)S(1)}, u32[]{:S(2)}, u32[]{:S(2)}) collective-permute-start(f32[32,1792]{1,0:T(8,128)S(1)} %get-tuple-element.23), channel_id=1, source_target_pairs={{0,64},{1,17},{2,66},{3,19},{4,68},{5,21},{6,70},{7,23},{8,72},{9,... | collective-permute-start | bytes 688136 | tf_op jit(solution)/shard_map/ppermute | solution.py:34
  41.9 8.0 %collective-permute-start.9 = (f32[32,1792]{1,0:T(8,128)S(1)}, f32[32,1792]{1,0:T(8,128)S(1)}, u32[]{:S(2)}, u32[]{:S(2)}) collective-permute-start(f32[32,1792]{1,0:T(8,128)S(1)} %get-tuple-element.23), channel_id=1, source_target_pairs={{0,32},{1,9},{2,34},{3,11},{4,36},{5,13},{6,38},{7,15},{8,40},{9,1... | collective-permute-start | bytes 688136 | tf_op jit(solution)/shard_map/ppermute | solution.py:34
  43.4 6.5 %collective-permute-start.12 = (f32[32,384]{1,0:T(8,128)S(1)}, f32[32,384]{1,0:T(8,128)S(1)}, u32[]{:S(2)}, u32[]{:S(2)}) collective-permute-start(f32[32,384]{1,0:T(8,128)S(1)} %get-tuple-element.24.mine_ref), channel_id=1, source_target_pairs={{0,8},{1,9},{2,10},{3,11},{4,12},{5,13},{6,14},{7,15},{8,0},{9,1},... | collective-permute-start | bytes 147464 | tf_op jit(solution)/shard_map/ppermute | solution.py:34
  49.9 9.8 %collective-permute-start.15 = (f32[32,1792]{1,0:T(8,128)S(1)}, f32[32,1792]{1,0:T(8,128)S(1)}, u32[]{:S(2)}, u32[]{:S(2)}) collective-permute-start(f32[32,1792]{1,0:T(8,128)S(1)} %add_add_fusion.1), channel_id=1, source_target_pairs={{0,24},{1,97},{2,26},{3,99},{4,28},{5,101},{6,30},{7,103},{8,16},{... | collective-permute-start | bytes 688136 | tf_op jit(solution)/shard_map/ppermute | solution.py:34
  53.7 7.5 %collective-permute-start.14 = (f32[32,1792]{1,0:T(8,128)S(1)}, f32[32,1792]{1,0:T(8,128)S(1)}, u32[]{:S(2)}, u32[]{:S(2)}) collective-permute-start(f32[32,1792]{1,0:T(8,128)S(1)} %add_add_fusion.1), channel_id=1, source_target_pairs={{0,16},{1,65},{2,18},{3,67},{4,20},{5,69},{6,22},{7,71},{8,24},{9,... | collective-permute-start | bytes 688136 | tf_op jit(solution)/shard_map/ppermute | solution.py:34
  53.7 7.5 %collective-permute-start.13 = (f32[32,1792]{1,0:T(8,128)S(1)}, f32[32,1792]{1,0:T(8,128)S(1)}, u32[]{:S(2)}, u32[]{:S(2)}) collective-permute-start(f32[32,1792]{1,0:T(8,128)S(1)} %add_add_fusion.1), channel_id=1, source_target_pairs={{0,8},{1,33},{2,10},{3,35},{4,12},{5,37},{6,14},{7,39},{8,0},{9,41... | collective-permute-start | bytes 688136 | tf_op jit(solution)/shard_map/ppermute | solution.py:34

commit v2 on v1

--- a/solution.py
+++ b/solution.py
@@ -8,35 +8,41 @@
 RING = 4
 BOTH = ("replica", "tensor")
 RANK = 32
+LEFT_CHUNK = 512
 CHUNK = 256
 STATE = 256
 HBM = pl.BlockSpec(memory_space=pltpu.HBM)
 VMEM = pl.BlockSpec(memory_space=pltpu.VMEM)
 
 
-def swap_pairs(even, odd):
+def role_of(x, y, core):
+    return (core + x // 2 + y // 2) % 2
+
+
+def pairs_of(specs, by_role):
     pairs = []
     for device in range(RING**3 * 2):
-        place = {
-            "c": device % 2,
-            "x": device // 2 % RING,
-            "z": device // (2 * RING) % RING,
-            "y": device // (2 * RING * RING),
-        }
-        axis, flip = (even, odd)[place["c"]]
-        place[axis] ^= flip
-        target = ((place["y"] * RING + place["z"]) * RING + place["x"]) * 2 + place["c"]
-        pairs.append((device, target))
+        core, x = device % 2, device // 2 % RING
+        z, y = device // (2 * RING) % RING, device // (2 * RING * RING)
+        kind = role_of(x, y, core) if by_role else core
+        axis, flip = specs[kind]
+        if axis == "c":
+            core ^= flip
+        else:
+            x, y, z = x ^ (flip * (axis == "x")), y ^ (flip * (axis == "y")), z ^ (flip * (axis == "z"))
+            if by_role:
+                core = role_of(x, y, kind)
+        pairs.append((device, ((y * RING + z) * RING + x) * 2 + core))
     return pairs
 
 
-def swap(value, even, odd=None):
-    return lax.ppermute(value, BOTH, swap_pairs(even, odd or even))
-
-
-def sum_four(value, even, odd):
-    one, two, three = (swap(value, (even, k), (odd, k)) for k in (1, 2, 3))
-    return (value + one) + (two + three)
+def swap(value, even, odd=None, by_role=False):
+    return lax.ppermute(value, BOTH, pairs_of((even, odd or even), by_role))
+
+
+def sum_four(value, even, odd, order, by_role=False):
+    parts = {k: swap(value, (even, k), (odd, k), by_role) for k in order}
+    return (value + parts[1]) + (parts[2] + parts[3])
 
 
 def split(value, count):
@@ -59,63 +65,107 @@
     return pltpu.CompilerParams(vmem_limit_bytes=mebibytes * 1024 * 1024)
 
 
-def core_of():
-    return lax.rem(lax.axis_index("tensor"), 2)
-
-
-def left_kernel(q_ref, error_hbm, change_hbm, send_ref, keep_ref, error_ref, change_ref, factor_ref, sems):
-    core = core_of()
+def own_role():
+    tensor, replica = lax.axis_index("tensor"), lax.axis_index("replica")
+    return lax.rem(lax.rem(tensor, 2) + tensor // 4 + replica // 8, 2)
+
+
+def left_terms(factor_ref, error_ref, change_ref, rows):
+    term = jnp.dot(error_ref[rows, :], factor_ref[...], preferred_element_type=jnp.float32)
+    term -= jnp.dot(change_ref[rows, :], factor_ref[...], preferred_element_type=jnp.float32)
+    return fold(term.T)
+
+
+def left_kernel(
+    q_hbm, error_hbm, change_hbm, send_ref, keep_ref, factor_ref, error_ref, change_ref, q_ref, q_sem, sems
+):
+    role = own_role()
     half = send_ref.shape[1]
-    count = 2 * half // CHUNK
+    count = 2 * half // LEFT_CHUNK
+    fetch = pltpu.make_async_copy(q_hbm, q_ref, q_sem)
+    fetch.start()
     blocks, copies = [], []
     for k in range(count):
-        side = (1 - core) if k < count // 2 else core
-        rows = pl.ds(pl.multiple_of(side * half + k % (count // 2) * CHUNK, CHUNK), CHUNK)
-        pair = [
+        side = (1 - role) if k < count // 2 else role
+        start = pl.multiple_of(side * half + k % (count // 2) * LEFT_CHUNK, LEFT_CHUNK)
+        rows = pl.ds(start, LEFT_CHUNK)
+        blocks.append(rows)
+        copies.append([
             pltpu.make_async_copy(source.at[rows], target.at[rows], sems.at[j, k])
             for j, (source, target) in enumerate(((error_hbm, error_ref), (change_hbm, change_ref)))
-        ]
-        for copy in pair:
-            copy.start()
-        blocks.append(rows)
-        copies.append(pair)
+        ])
+
+    def begin(k):
+        if k < count:
+            for copy in copies[k]:
+                copy.start()
+
+    begin(0)
+    fetch.wait()
+    begin(1)
     parts = [part.astype(jnp.float32) for part in split(q_ref[...], 3)]
     stacked = jnp.concatenate(parts + [jnp.zeros_like(parts[0])], axis=0)
     factor_ref[...] = stacked.T.astype(jnp.bfloat16)
     for k in range(count):
         for copy in copies[k]:
             copy.wait()
-        term = jnp.dot(error_ref[blocks[k], :], factor_ref[...], preferred_element_type=jnp.float32)
-        term -= jnp.dot(change_ref[blocks[k], :], factor_ref[...], preferred_element_type=jnp.float32)
-        target = send_ref if k < count // 2 else keep_ref
-        start = k % (count // 2) * CHUNK
-        target[:, start : start + CHUNK] = fold(term.T)
+        begin(k + 2)
+        if k < count // 2:
+            send_ref[:, k * LEFT_CHUNK : (k + 1) * LEFT_CHUNK] = left_terms(
+                factor_ref, error_ref, change_ref, blocks[k]
+            )
+        elif k < count - 1:
+            start = (k - count // 2) * LEFT_CHUNK
+            keep_ref[:, start : start + LEFT_CHUNK] = left_terms(factor_ref, error_ref, change_ref, blocks[k])
+
+
+def rest_kernel(factor_ref, error_ref, change_ref, keep_ref, out_ref):
+    half = out_ref.shape[1]
+    done = half - LEFT_CHUNK
+    out_ref[:, :done] = keep_ref[...]
+    rows = pl.ds(pl.multiple_of(own_role() * half + done, LEFT_CHUNK), LEFT_CHUNK)
+    out_ref[:, done:] = left_terms(factor_ref, error_ref, change_ref, rows)
 
 
 def left_factor(q_prev, error_memory, inner_change):
     rows, columns = error_memory.shape
     half = rows // 2
-    return pl.pallas_call(
+    send, keep, factor, error, change = pl.pallas_call(
         left_kernel,
-        in_specs=[VMEM, HBM, HBM],
-        out_specs=[VMEM] * 4,
+        in_specs=[HBM, HBM, HBM],
+        out_specs=[VMEM] * 5,
         out_shape=[
             pltpu.VMEM((RANK, half), jnp.float32),
-            pltpu.VMEM((RANK, half), jnp.float32),
+            pltpu.VMEM((RANK, half - LEFT_CHUNK), jnp.float32),
+            pltpu.VMEM((columns, 4 * RANK), jnp.bfloat16),
             pltpu.VMEM((rows, columns), jnp.bfloat16),
             pltpu.VMEM((rows, columns), jnp.bfloat16),
         ],
         scratch_shapes=[
-            pltpu.VMEM((columns, 4 * RANK), jnp.bfloat16),
-            pltpu.SemaphoreType.DMA((2, rows // CHUNK)),
+            pltpu.VMEM((RANK, columns), jnp.float32),
+            pltpu.SemaphoreType.DMA,
+            pltpu.SemaphoreType.DMA((2, rows // LEFT_CHUNK)),
         ],
         compiler_params=params(8),
         cost_estimate=pl.CostEstimate(
             flops=12 * RANK * rows * columns, bytes_accessed=4 * rows * columns, transcendentals=0
         ),
         name="left_factor",
-    )(q_prev, pltpu.with_memory_space_constraint(error_memory, pltpu.HBM),
-      pltpu.with_memory_space_constraint(inner_change, pltpu.HBM))
+    )(*(pltpu.with_memory_space_constraint(value, pltpu.HBM) for value in (q_prev, error_memory, inner_change)))
+    keep = pl.pallas_call(
+        rest_kernel,
+        in_specs=[VMEM] * 4,
+        out_specs=VMEM,
+        out_shape=pltpu.VMEM((RANK, half), jnp.float32),
+        compiler_params=params(8),
+        cost_estimate=pl.CostEstimate(
+            flops=12 * RANK * LEFT_CHUNK * columns,
+            bytes_accessed=4 * LEFT_CHUNK * columns,
+            transcendentals=0,
+        ),
+        name="left_rest",
+    )(factor, error, change, keep)
+    return send, keep, error, change
 
 
 def right_products(left_ref, error_ref, change_ref, side, previous_ref, out_ref):
@@ -135,19 +185,19 @@
 
 
 def first_kernel(own_ref, error_ref, change_ref, out_ref, gram_ref):
-    gram = right_products(own_ref, error_ref, change_ref, core_of(), None, out_ref)
+    gram = right_products(own_ref, error_ref, change_ref, own_role(), None, out_ref)
     gram_ref[...] = jnp.concatenate([gram, jnp.zeros((RANK, 128 - RANK), jnp.float32)], axis=1)
 
 
 def second_kernel(own_ref, other_ref, error_ref, change_ref, previous_ref, gram_ref, out_ref, whole_ref, share_ref):
-    core = core_of()
+    role = own_role()
     half = own_ref.shape[1]
-    gram = right_products(other_ref, error_ref, change_ref, 1 - core, previous_ref, out_ref)
+    gram = right_products(other_ref, error_ref, change_ref, 1 - role, previous_ref, out_ref)
     share_ref[:, :128] = gram_ref[...] + jnp.concatenate(
         [gram, jnp.zeros((RANK, 128 - RANK), jnp.float32)], axis=1
     )
-    whole_ref[:, pl.ds(pl.multiple_of(core * half, half), half)] = own_ref[...]
-    whole_ref[:, pl.ds(pl.multiple_of((1 - core) * half, half), half)] = other_ref[...]
+    whole_ref[:, pl.ds(pl.multiple_of(role * half, half), half)] = own_ref[...]
+    whole_ref[:, pl.ds(pl.multiple_of((1 - role) * half, half), half)] = other_ref[...]
     position = lax.axis_index("replica")
     neighbour = position + 1 - 2 * lax.rem(position, 2)
     start = lax.rem(neighbour, 8) * STATE
@@ -248,8 +298,9 @@
     top, low = split(new_q, 2)
     factor = jnp.concatenate([top, top, low, low], axis=0)
     started = []
-    for k in range(rows // CHUNK):
-        block = pl.ds(k * CHUNK, CHUNK)
+    starts = [0, CHUNK // 2, *range(CHUNK, rows, CHUNK), rows]
+    for k, (start, end) in enumerate(zip(starts, starts[1:])):
+        block = pl.ds(start, end - start)
         approx = jnp.dot(basis_ref[block, :], factor, preferred_element_type=jnp.float32)
         combined = error_ref[block, :].astype(jnp.float32) - change_ref[block, :].astype(jnp.float32)
         error_out_ref[block, :] = (combined - approx).astype(jnp.bfloat16)
@@ -287,7 +338,7 @@
             pltpu.VMEM(state, jnp.float32),
             pltpu.VMEM(state, jnp.bfloat16),
             pltpu.VMEM((rows, columns), jnp.bfloat16),
-            pltpu.SemaphoreType.DMA((2 + rows // CHUNK,)),
+            pltpu.SemaphoreType.DMA((3 + rows // CHUNK,)),
         ],
         compiler_params=params(18),
         cost_estimate=pl.CostEstimate(
@@ -302,17 +353,17 @@
 
     send, keep, error, change = left_factor(q_prev, error_memory, inner_change)
     own = keep + swap(send, ("c", 1))
-    own = sum_four(own, "x", "y")
-    own = sum_four(own, "y", "x")
-    own = own + swap(own, ("z", 2))
+    own = sum_four(own, "x", "y", (1, 3, 2), by_role=True)
+    own = own + swap(own, ("z", 2), by_role=True)
+    own = sum_four(own, "y", "x", (1, 3, 2), by_role=True)
     other = swap(own, ("c", 1))
 
     projected, whole, mine = right_factor(own, other, error, change)
     theirs = swap(mine, ("z", 1))
-    summed = sum_four(projected, "y", "z")
+    summed = sum_four(projected, "y", "z", (3, 1, 2))
     summed, theirs = lax.optimization_barrier((summed, theirs))
     inverse, basis = make_basis(whole, mine, theirs)
-    summed = sum_four(summed, "z", "y")
+    summed = sum_four(summed, "z", "y", (3, 1, 2))
     update, new_momentum, new_error, new_q = apply_factors(
         replicas, summed, inverse, basis, error, change, momentum
     )

time: 66.8 us -> 63.5 us (0.951)
  starting transfers between devices: 22.9 us -> 21.6 us
  local copies, waits for them, and re-layouts: 0.94 us -> 0.01 us
  waiting for transfers between devices: 23.3 us -> 22.4 us
    ppermute x16, starting transfers between devices: 22.9 us -> 21.6 us  [swap(): return lax.ppermute(value, BOTH, pairs_of((even, odd or even), by_role))]
    unnamed x4 -> x2, local copies, waits for them, and re-layouts: 0.94 us -> 0.01 us
    ppermute x16, waiting for transfers between devices: 23.3 us -> 22.4 us  [swap(): return lax.ppermute(value, BOTH, pairs_of((even, odd or even), by_role))]
    pallas_call x1 -> x2, Pallas kernels: 7.24 us -> 7.06 us  [the longest x1 5.89 us: left_factor(): pl.pallas_call(left_kernel, in_specs=[HBM, HBM, HBM], out_specs=[VMEM] *...]
  transfers between devices with their start and end apart: 16 -> 16, of which waited for: 10 -> 11; matrix products, arithmetic and copies ran while one was open for 0% -> 0% of each run, Pallas kernels for 7% -> 9%
where the time goes in v2:
time: 63.5 us; the launch traced here: 63.4 us
  waiting for transfers between devices  22.4 us (35%)
  starting transfers between devices  21.6 us (34%)
  Pallas kernels  18.3 us (29%)
  between operations  0.9 us (1%)
    ppermute x16, waiting for transfers between devices, swap(): return lax.ppermute(value, BOTH, pairs_of((even, odd or even), by_role))  22.4 us
    ppermute x16, starting transfers between devices, swap(): return lax.ppermute(value, BOTH, pairs_of((even, odd or even), by_role))  21.6 us
    pallas_call x1, Pallas kernels, left_factor(): pl.pallas_call(left_kernel, in_specs=[HBM, HBM, HBM], out_specs=[VMEM] *...  5.89 us
    pallas_call x1, Pallas kernels, apply_factors(): pl.pallas_call(lambda *refs: apply_kernel(count, *refs), in_specs=[VMEM]...  5.22 us
    pallas_call x1, Pallas kernels, make_basis(): pl.pallas_call(basis_kernel, in_specs=[VMEM] * 3, out_specs=[VMEM, VMEM],...  3.13 us
    pallas_call x1, Pallas kernels, right_factor(): pl.pallas_call(second_kernel, in_specs=[VMEM] * 6, out_specs=[VMEM] * 3,...  1.44 us
    pallas_call x1, Pallas kernels, right_factor(): pl.pallas_call(first_kernel, in_specs=[VMEM] * 3, out_specs=[VMEM] * 2, o...  1.44 us
  transfers between devices with their start and end apart: 16, of which 11 were waited for; matrix products, arithmetic and copies ran while one was open for 0% of the time, Pallas kernels for 9%

profile of v2, /device:TPU:0, one launch (start us, length us, event | category | flops | bytes accessed | tf_op | source)
XLA Modules:
  0.0 63.4 jit_solution(6496350128746481150)
XLA Ops:
  0.6 5.9 %left_factor.1 = (f32[32,1024]{1,0:T(8,128)S(1)}, f32[32,512]{1,0:T(8,128)S(1)}, bf16[1792,128]{1,0:T(8,128)(2,1)S(1)}, bf16[2048,1792]{1,0:T(8,128)(2,1)S(1)}, bf16[2048,1792]{1,0:T(8,128)(2,1)S(1)}) custom-call(f32[32,1792]{1,0:T(8,128)} %q_hbm.1, bf16[2048,1792]{1,0:T(8,128)(2,1)} %error_hbm.1, bf16[2048,1792]{1,0:T(8,128)(2,1)} %change_hbm.1), custom_call_target="tpu_custom_call" | custom-call | flops 1409286144 | bytes 14680064 | tf_op jit(solution)/shard_map/left_factor/pallas_call | solution.py:133
  6.6 1.2 %left_rest.1 = f32[32,1024]{1,0:T(8,128)S(1)} custom-call(bf16[1792,128]{1,0:T(8,128)(2,1)S(1)} %get-tuple-element.18.factor_ref, bf16[2048,1792]{1,0:T(8,128)(2,1)S(1)} %get-tuple-element.19.error_ref.refs_3_, bf16[2048,1792]{1,0:T(8,128)(2,1)S(1)} %get-tuple-element.20.change_ref.refs_4_, f32[32,512]{1,0:T(8,128)S(1)} %get-tuple-element.21.keep_ref), custom_call_target="tpu_custom_call" | custom-call | flops 352321536 | bytes 3670016 | tf_op jit(solution)/shard_map/left_rest/pallas_call | solution.py:155
  8.0 2.9 %collective-permute-start.3 = (f32[32,1024]{1,0:T(8,128)S(1)}, f32[32,1024]{1,0:T(8,128)S(1)}, u32[]{:S(2)}, u32[]{:S(2)}) collective-permute-start(f32[32,1024]{1,0:T(8,128)S(1)} %add.42), channel_id=1, source_target_pairs={{0,7},{1,96},{2,5},{3,98},{4,101},{5,2},{6,103},{7,0},{8,15},{9,10... | collective-permute-start | bytes 393224 | tf_op jit(solution)/shard_map/ppermute | solution.py:40
  11.9 2.9 %collective-permute-done.3 = f32[32,1024]{1,0:T(8,128)S(1)} collective-permute-done((f32[32,1024]{1,0:T(8,128)S(1)}, f32[32,1024]{1,0:T(8,128)S(1)}, u32[]{:S(2)}, u32[]{:S(2)}) %collective-permute-start.3) | collective-permute-done | bytes 131104 | tf_op jit(solution)/shard_map/ppermute | solution.py:40
  14.8 2.0 %collective-permute-done.2 = f32[32,1024]{1,0:T(8,128)S(1)} collective-permute-done((f32[32,1024]{1,0:T(8,128)S(1)}, f32[32,1024]{1,0:T(8,128)S(1)}, u32[]{:S(2)}, u32[]{:S(2)}) %collective-permute-start.2) | collective-permute-done | bytes 131104 | tf_op jit(solution)/shard_map/ppermute | solution.py:40
  16.8 4.0 %collective-permute-start.4 = (f32[32,1024]{1,0:T(8,128)S(1)}, f32[32,1024]{1,0:T(8,128)S(1)}, u32[]{:S(2)}, u32[]{:S(2)}) collective-permute-start(f32[32,1024]{1,0:T(8,128)S(1)} %add_add_fusion.3), channel_id=1, source_target_pairs={{0,16},{1,17},{2,18},{3,19},{4,20},{5,21},{6,22},{7,23},{8,24},{9,... | collective-permute-start | bytes 393224 | tf_op jit(solution)/shard_map/ppermute | solution.py:40
  20.7 4.1 %collective-permute-done.4 = f32[32,1024]{1,0:T(8,128)S(1)} collective-permute-done((f32[32,1024]{1,0:T(8,128)S(1)}, f32[32,1024]{1,0:T(8,128)S(1)}, u32[]{:S(2)}, u32[]{:S(2)}) %collective-permute-start.4) | collective-permute-done | bytes 131104 | tf_op jit(solution)/shard_map/ppermute | solution.py:40
  24.8 2.5 %collective-permute-start.7 = (f32[32,1024]{1,0:T(8,128)S(1)}, f32[32,1024]{1,0:T(8,128)S(1)}, u32[]{:S(2)}, u32[]{:S(2)}) collective-permute-start(f32[32,1024]{1,0:T(8,128)S(1)} %add.46), channel_id=1, source_target_pairs={{0,97},{1,6},{2,99},{3,4},{4,3},{5,100},{6,1},{7,102},{8,105},{9,1... | collective-permute-start | bytes 393224 | tf_op jit(solution)/shard_map/ppermute | solution.py:40
  27.6 1.1 %collective-permute-start.5 = (f32[32,1024]{1,0:T(8,128)S(1)}, f32[32,1024]{1,0:T(8,128)S(1)}, u32[]{:S(2)}, u32[]{:S(2)}) collective-permute-start(f32[32,1024]{1,0:T(8,128)S(1)} %add.46), channel_id=1, source_target_pairs={{0,32},{1,3},{2,34},{3,1},{4,6},{5,37},{6,4},{7,39},{8,40},{9,11},... | collective-permute-start | bytes 393224 | tf_op jit(solution)/shard_map/ppermute | solution.py:40
  28.7 2.5 %collective-permute-done.7 = f32[32,1024]{1,0:T(8,128)S(1)} collective-permute-done((f32[32,1024]{1,0:T(8,128)S(1)}, f32[32,1024]{1,0:T(8,128)S(1)}, u32[]{:S(2)}, u32[]{:S(2)}) %collective-permute-start.7) | collective-permute-done | bytes 131104 | tf_op jit(solution)/shard_map/ppermute | solution.py:40
  31.3 2.0 %collective-permute-done.6 = f32[32,1024]{1,0:T(8,128)S(1)} collective-permute-done((f32[32,1024]{1,0:T(8,128)S(1)}, f32[32,1024]{1,0:T(8,128)S(1)}, u32[]{:S(2)}, u32[]{:S(2)}) %collective-permute-start.6) | collective-permute-done | bytes 131104 | tf_op jit(solution)/shard_map/ppermute | solution.py:40
  33.4 1.4 %right_first.1 = (f32[32,1792]{1,0:T(8,128)S(1)}, f32[32,128]{1,0:T(8,128)S(1)}) custom-call(f32[32,1024]{1,0:T(8,128)S(1)} %add_add_fusion.2.own_ref, bf16[2048,1792]{1,0:T(8,128)(2,1)S(1)} %get-tuple-element.19.error_ref.refs_3_, bf16[2048,1792]{1,0:T(8,128)(2,1)S(1)} %get-tuple-element.20.change_ref.refs_4_), custom_call_target="tpu_custom_call" | custom-call | flops 704643072 | bytes 7340032 | tf_op jit(solution)/shard_map/right_first/pallas_call | solution.py:213
  34.8 1.4 %right_second.1 = (f32[32,1792]{1,0:T(8,128)S(1)}, f32[32,2048]{1,0:T(8,128)S(1)}, f32[32,384]{1,0:T(8,128)S(1)}) custom-call(f32[32,1024]{1,0:T(8,128)S(1)} %add_add_fusion.2.own_ref, f32[32,1024]{1,0:T(8,128)S(1)} %collective-permute-done.8.other_ref, bf16[2048,1792]{1,0:T(8,128)(2,1)S(1)} %get-tuple-element.19.error_ref.refs_3_, ...), custom_call_target="tpu_custom_call" | custom-call | flops 704643072 | bytes 7340032 | tf_op jit(solution)/shard_map/right_second/pallas_call | solution.py:225
  36.3 2.7 %collective-permute-start.11 = (f32[32,1792]{1,0:T(8,128)S(1)}, f32[32,1792]{1,0:T(8,128)S(1)}, u32[]{:S(2)}, u32[]{:S(2)}) collective-permute-start(f32[32,1792]{1,0:T(8,128)S(1)} %get-tuple-element.25), channel_id=1, source_target_pairs={{0,96},{1,25},{2,98},{3,27},{4,100},{5,29},{6,102},{7,31},{8,104},... | collective-permute-start | bytes 688136 | tf_op jit(solution)/shard_map/ppermute | solution.py:40
  39.3 1.1 %collective-permute-start.9 = (f32[32,1792]{1,0:T(8,128)S(1)}, f32[32,1792]{1,0:T(8,128)S(1)}, u32[]{:S(2)}, u32[]{:S(2)}) collective-permute-start(f32[32,1792]{1,0:T(8,128)S(1)} %get-tuple-element.25), channel_id=1, source_target_pairs={{0,32},{1,9},{2,34},{3,11},{4,36},{5,13},{6,38},{7,15},{8,40},{9,1... | collective-permute-start | bytes 688136 | tf_op jit(solution)/shard_map/ppermute | solution.py:40
  40.4 1.2 %collective-permute-start.12 = (f32[32,384]{1,0:T(8,128)S(1)}, f32[32,384]{1,0:T(8,128)S(1)}, u32[]{:S(2)}, u32[]{:S(2)}) collective-permute-start(f32[32,384]{1,0:T(8,128)S(1)} %get-tuple-element.26.mine_ref), channel_id=1, source_target_pairs={{0,8},{1,9},{2,10},{3,11},{4,12},{5,13},{6,14},{7,15},{8,0},{9,1},... | collective-permute-start | bytes 147464 | tf_op jit(solution)/shard_map/ppermute | solution.py:40
  41.6 3.3 %collective-permute-done.11 = f32[32,1792]{1,0:T(8,128)S(1)} collective-permute-done((f32[32,1792]{1,0:T(8,128)S(1)}, f32[32,1792]{1,0:T(8,128)S(1)}, u32[]{:S(2)}, u32[]{:S(2)}) %collective-permute-start.11) | collective-permute-done | bytes 229408 | tf_op jit(solution)/shard_map/ppermute | solution.py:40
  45.0 1.5 %collective-permute-done.10 = f32[32,1792]{1,0:T(8,128)S(1)} collective-permute-done((f32[32,1792]{1,0:T(8,128)S(1)}, f32[32,1792]{1,0:T(8,128)S(1)}, u32[]{:S(2)}, u32[]{:S(2)}) %collective-permute-start.10) | collective-permute-done | bytes 229408 | tf_op jit(solution)/shard_map/ppermute | solution.py:40
  47.0 3.4 %collective-permute-start.15 = (f32[32,1792]{1,0:T(8,128)S(1)}, f32[32,1792]{1,0:T(8,128)S(1)}, u32[]{:S(2)}, u32[]{:S(2)}) collective-permute-start(f32[32,1792]{1,0:T(8,128)S(1)} %add_add_fusion.1), channel_id=1, source_target_pairs={{0,24},{1,97},{2,26},{3,99},{4,28},{5,101},{6,30},{7,103},{8,16},{... | collective-permute-start | bytes 688136 | tf_op jit(solution)/shard_map/ppermute | solution.py:40
  50.4 0.9 %collective-permute-start.13 = (f32[32,1792]{1,0:T(8,128)S(1)}, f32[32,1792]{1,0:T(8,128)S(1)}, u32[]{:S(2)}, u32[]{:S(2)}) collective-permute-start(f32[32,1792]{1,0:T(8,128)S(1)} %add_add_fusion.1), channel_id=1, source_target_pairs={{0,8},{1,33},{2,10},{3,35},{4,12},{5,37},{6,14},{7,39},{8,0},{9,41... | collective-permute-start | bytes 688136 | tf_op jit(solution)/shard_map/ppermute | solution.py:40
  51.3 3.1 %basis.1 = (f32[32,128]{1,0:T(8,128)S(1)}, bf16[2304,128]{1,0:T(8,128)(2,1)S(1)}) custom-call(f32[32,2048]{1,0:T(8,128)S(1)} %get-tuple-element.28.whole_ref, f32[32,384]{1,0:T(8,128)S(1)} %get-tuple-element.26.mine_ref, f32[32,384]{1,0:T(8,128)S(1)} %collective-permute-done.12.theirs_ref), custom_call_target="tpu_custom_call" | custom-call | flops 50331648 | bytes 1048576 | tf_op jit(solution)/shard_map/basis/pallas_call | solution.py:268
  54.5 1.9 %collective-permute-done.15 = f32[32,1792]{1,0:T(8,128)S(1)} collective-permute-done((f32[32,1792]{1,0:T(8,128)S(1)}, f32[32,1792]{1,0:T(8,128)S(1)}, u32[]{:S(2)}, u32[]{:S(2)}) %collective-permute-start.15) | collective-permute-done | bytes 229408 | tf_op jit(solution)/shard_map/ppermute | solution.py:40
  56.4 1.5 %collective-permute-done.14 = f32[32,1792]{1,0:T(8,128)S(1)} collective-permute-done((f32[32,1792]{1,0:T(8,128)S(1)}, f32[32,1792]{1,0:T(8,128)S(1)}, u32[]{:S(2)}, u32[]{:S(2)}) %collective-permute-start.14) | collective-permute-done | bytes 229408 | tf_op jit(solution)/shard_map/ppermute | solution.py:40
  58.0 5.2 %apply.1 = (bf16[256,1792]{1,0:T(8,128)(2,1)}, f32[256,1792]{1,0:T(8,128)}, bf16[2048,1792]{1,0:T(8,128)(2,1)}, f32[32,1792]{1,0:T(8,128)}) custom-call(f32[32,1792]{1,0:T(8,128)S(1)} %add_add_fusion.refs_0_, f32[32,128]{1,0:T(8,128)S(1)} %get-tuple-element.30.refs_1_, bf16[2304,128]{1,0:T(8,128)(2,1)S(1)} %get-tuple-element.31.refs_2_, ...), custom_call_target="tpu_custom_call" | custom-call | flops 939524096 | bytes 22020096 | tf_op jit(solution)/shard_map/apply/pallas_call | solution.py:327
  (22 shorter events, 2.7 us)
Async XLA Ops:
  6.5 1.4 %collective-permute-start = (f32[32,1024]{1,0:T(8,128)S(1)}, f32[32,1024]{1,0:T(8,128)S(1)}, u32[]{:S(2)}, u32[]{:S(2)}) collective-permute-start(f32[32,1024]{1,0:T(8,128)S(1)} %get-tuple-element.22), channel_id=1, source_target_pairs={{0,1},{1,0},{2,3},{3,2},{4,5},{5,4},{6,7},{7,6},{8,9},{9,8},{10,11... | collective-permute-start | bytes 393224 | tf_op jit(solution)/shard_map/ppermute | solution.py:40
  8.0 6.8 %collective-permute-start.3 = (f32[32,1024]{1,0:T(8,128)S(1)}, f32[32,1024]{1,0:T(8,128)S(1)}, u32[]{:S(2)}, u32[]{:S(2)}) collective-permute-start(f32[32,1024]{1,0:T(8,128)S(1)} %add.42), channel_id=1, source_target_pairs={{0,7},{1,96},{2,5},{3,98},{4,101},{5,2},{6,103},{7,0},{8,15},{9,10... | collective-permute-start | bytes 393224 | tf_op jit(solution)/shard_map/ppermute | solution.py:40
  10.9 5.9 %collective-permute-start.2 = (f32[32,1024]{1,0:T(8,128)S(1)}, f32[32,1024]{1,0:T(8,128)S(1)}, u32[]{:S(2)}, u32[]{:S(2)}) collective-permute-start(f32[32,1024]{1,0:T(8,128)S(1)} %add.42), channel_id=1, source_target_pairs={{0,5},{1,64},{2,7},{3,66},{4,69},{5,0},{6,71},{7,2},{8,13},{9,72},... | collective-permute-start | bytes 393224 | tf_op jit(solution)/shard_map/ppermute | solution.py:40
  11.4 5.3 %collective-permute-start.1 = (f32[32,1024]{1,0:T(8,128)S(1)}, f32[32,1024]{1,0:T(8,128)S(1)}, u32[]{:S(2)}, u32[]{:S(2)}) collective-permute-start(f32[32,1024]{1,0:T(8,128)S(1)} %add.42), channel_id=1, source_target_pairs={{0,2},{1,33},{2,0},{3,35},{4,36},{5,7},{6,38},{7,5},{8,10},{9,41},... | collective-permute-start | bytes 393224 | tf_op jit(solution)/shard_map/ppermute | solution.py:40
  16.8 8.0 %collective-permute-start.4 = (f32[32,1024]{1,0:T(8,128)S(1)}, f32[32,1024]{1,0:T(8,128)S(1)}, u32[]{:S(2)}, u32[]{:S(2)}) collective-permute-start(f32[32,1024]{1,0:T(8,128)S(1)} %add_add_fusion.3), channel_id=1, source_target_pairs={{0,16},{1,17},{2,18},{3,19},{4,20},{5,21},{6,22},{7,23},{8,24},{9,... | collective-permute-start | bytes 393224 | tf_op jit(solution)/shard_map/ppermute | solution.py:40
  24.8 6.4 %collective-permute-start.7 = (f32[32,1024]{1,0:T(8,128)S(1)}, f32[32,1024]{1,0:T(8,128)S(1)}, u32[]{:S(2)}, u32[]{:S(2)}) collective-permute-start(f32[32,1024]{1,0:T(8,128)S(1)} %add.46), channel_id=1, source_target_pairs={{0,97},{1,6},{2,99},{3,4},{4,3},{5,100},{6,1},{7,102},{8,105},{9,1... | collective-permute-start | bytes 393224 | tf_op jit(solution)/shard_map/ppermute | solution.py:40
  27.3 5.9 %collective-permute-start.6 = (f32[32,1024]{1,0:T(8,128)S(1)}, f32[32,1024]{1,0:T(8,128)S(1)}, u32[]{:S(2)}, u32[]{:S(2)}) collective-permute-start(f32[32,1024]{1,0:T(8,128)S(1)} %add.46), channel_id=1, source_target_pairs={{0,65},{1,4},{2,67},{3,6},{4,1},{5,68},{6,3},{7,70},{8,73},{9,12},... | collective-permute-start | bytes 393224 | tf_op jit(solution)/shard_map/ppermute | solution.py:40
  27.6 5.6 %collective-permute-start.5 = (f32[32,1024]{1,0:T(8,128)S(1)}, f32[32,1024]{1,0:T(8,128)S(1)}, u32[]{:S(2)}, u32[]{:S(2)}) collective-permute-start(f32[32,1024]{1,0:T(8,128)S(1)} %add.46), channel_id=1, source_target_pairs={{0,32},{1,3},{2,34},{3,1},{4,6},{5,37},{6,4},{7,39},{8,40},{9,11},... | collective-permute-start | bytes 393224 | tf_op jit(solution)/shard_map/ppermute | solution.py:40
  33.3 1.5 %collective-permute-start.8 = (f32[32,1024]{1,0:T(8,128)S(1)}, f32[32,1024]{1,0:T(8,128)S(1)}, u32[]{:S(2)}, u32[]{:S(2)}) collective-permute-start(f32[32,1024]{1,0:T(8,128)S(1)} %add_add_fusion.2.own_ref), channel_id=1, source_target_pairs={{0,1},{1,0},{2,3},{3,2},{4,5},{5,4},{6,7},{7,6},{8,9},{9,8},{10,11... | collective-permute-start | bytes 393224 | tf_op jit(solution)/shard_map/ppermute | solution.py:40
  34.8 23.2 %copy-start = (f32[256,1792]{1,0:T(8,128)S(1)}, f32[256,1792]{1,0:T(8,128)}, u32[]{:S(2)}) copy-start(f32[256,1792]{1,0:T(8,128)} %refs_5_.1) | copy-start | bytes 5505028
  36.3 8.7 %collective-permute-start.11 = (f32[32,1792]{1,0:T(8,128)S(1)}, f32[32,1792]{1,0:T(8,128)S(1)}, u32[]{:S(2)}, u32[]{:S(2)}) collective-permute-start(f32[32,1792]{1,0:T(8,128)S(1)} %get-tuple-element.25), channel_id=1, source_target_pairs={{0,96},{1,25},{2,98},{3,27},{4,100},{5,29},{6,102},{7,31},{8,104},... | collective-permute-start | bytes 688136 | tf_op jit(solution)/shard_map/ppermute | solution.py:40
  39.0 7.5 %collective-permute-start.10 = (f32[32,1792]{1,0:T(8,128)S(1)}, f32[32,1792]{1,0:T(8,128)S(1)}, u32[]{:S(2)}, u32[]{:S(2)}) collective-permute-start(f32[32,1792]{1,0:T(8,128)S(1)} %get-tuple-element.25), channel_id=1, source_target_pairs={{0,64},{1,17},{2,66},{3,19},{4,68},{5,21},{6,70},{7,23},{8,72},{9,... | collective-permute-start | bytes 688136 | tf_op jit(solution)/shard_map/ppermute | solution.py:40
  39.3 7.6 %collective-permute-start.9 = (f32[32,1792]{1,0:T(8,128)S(1)}, f32[32,1792]{1,0:T(8,128)S(1)}, u32[]{:S(2)}, u32[]{:S(2)}) collective-permute-start(f32[32,1792]{1,0:T(8,128)S(1)} %get-tuple-element.25), channel_id=1, source_target_pairs={{0,32},{1,9},{2,34},{3,11},{4,36},{5,13},{6,38},{7,15},{8,40},{9,1... | collective-permute-start | bytes 688136 | tf_op jit(solution)/shard_map/ppermute | solution.py:40
  40.4 6.5 %collective-permute-start.12 = (f32[32,384]{1,0:T(8,128)S(1)}, f32[32,384]{1,0:T(8,128)S(1)}, u32[]{:S(2)}, u32[]{:S(2)}) collective-permute-start(f32[32,384]{1,0:T(8,128)S(1)} %get-tuple-element.26.mine_ref), channel_id=1, source_target_pairs={{0,8},{1,9},{2,10},{3,11},{4,12},{5,13},{6,14},{7,15},{8,0},{9,1},... | collective-permute-start | bytes 147464 | tf_op jit(solution)/shard_map/ppermute | solution.py:40
  47.0 9.4 %collective-permute-start.15 = (f32[32,1792]{1,0:T(8,128)S(1)}, f32[32,1792]{1,0:T(8,128)S(1)}, u32[]{:S(2)}, u32[]{:S(2)}) collective-permute-start(f32[32,1792]{1,0:T(8,128)S(1)} %add_add_fusion.1), channel_id=1, source_target_pairs={{0,24},{1,97},{2,26},{3,99},{4,28},{5,101},{6,30},{7,103},{8,16},{... | collective-permute-start | bytes 688136 | tf_op jit(solution)/shard_map/ppermute | solution.py:40
  50.4 7.5 %collective-permute-start.14 = (f32[32,1792]{1,0:T(8,128)S(1)}, f32[32,1792]{1,0:T(8,128)S(1)}, u32[]{:S(2)}, u32[]{:S(2)}) collective-permute-start(f32[32,1792]{1,0:T(8,128)S(1)} %add_add_fusion.1), channel_id=1, source_target_pairs={{0,16},{1,65},{2,18},{3,67},{4,20},{5,69},{6,22},{7,71},{8,24},{9,... | collective-permute-start | bytes 688136 | tf_op jit(solution)/shard_map/ppermute | solution.py:40
  50.4 7.5 %collective-permute-start.13 = (f32[32,1792]{1,0:T(8,128)S(1)}, f32[32,1792]{1,0:T(8,128)S(1)}, u32[]{:S(2)}, u32[]{:S(2)}) collective-permute-start(f32[32,1792]{1,0:T(8,128)S(1)} %add_add_fusion.1), channel_id=1, source_target_pairs={{0,8},{1,33},{2,10},{3,35},{4,12},{5,37},{6,14},{7,39},{8,0},{9,41... | collective-permute-start | bytes 688136 | tf_op jit(solution)/shard_map/ppermute | solution.py:40

commit v3 on v2

--- a/solution.py
+++ b/solution.py
@@ -180,61 +180,67 @@
         if previous_ref is not None:
             value = value + previous_ref[:, block]
         out_ref[:, block] = value
-    squares = fold(lax.dot_general(factor, factor, NT, preferred_element_type=jnp.float32))
-    return (squares[:, :RANK] + squares[:, RANK : 2 * RANK]) + squares[:, 2 * RANK :]
-
-
-def first_kernel(own_ref, error_ref, change_ref, out_ref, gram_ref):
-    gram = right_products(own_ref, error_ref, change_ref, own_role(), None, out_ref)
-    gram_ref[...] = jnp.concatenate([gram, jnp.zeros((RANK, 128 - RANK), jnp.float32)], axis=1)
-
-
-def second_kernel(own_ref, other_ref, error_ref, change_ref, previous_ref, gram_ref, out_ref, whole_ref, share_ref):
+
+
+def first_kernel(own_ref, error_ref, change_ref, out_ref):
+    right_products(own_ref, error_ref, change_ref, own_role(), None, out_ref)
+
+
+def second_kernel(other_ref, error_ref, change_ref, previous_ref, out_ref):
+    right_products(other_ref, error_ref, change_ref, 1 - own_role(), previous_ref, out_ref)
+
+
+def right_factor(own, other, error, change):
+    rows, columns = error.shape
+    half = own.shape[1]
+    projected = None
+    for kernel, left in ((first_kernel, own), (second_kernel, other)):
+        more = [] if projected is None else [projected]
+        projected = pl.pallas_call(
+            kernel,
+            in_specs=[VMEM] * (3 + len(more)),
+            out_specs=VMEM,
+            out_shape=pltpu.VMEM((RANK, columns), jnp.float32),
+            compiler_params=params(8),
+            cost_estimate=pl.CostEstimate(
+                flops=12 * RANK * half * columns, bytes_accessed=4 * half * columns, transcendentals=0
+            ),
+            name="right_second" if more else "right_first",
+        )(left, error, change, *more)
+    return projected
+
+
+def share_kernel(own_ref, other_ref, whole_ref, share_ref):
     role = own_role()
     half = own_ref.shape[1]
-    gram = right_products(other_ref, error_ref, change_ref, 1 - role, previous_ref, out_ref)
-    share_ref[:, :128] = gram_ref[...] + jnp.concatenate(
-        [gram, jnp.zeros((RANK, 128 - RANK), jnp.float32)], axis=1
-    )
     whole_ref[:, pl.ds(pl.multiple_of(role * half, half), half)] = own_ref[...]
     whole_ref[:, pl.ds(pl.multiple_of((1 - role) * half, half), half)] = other_ref[...]
+    factor = jnp.concatenate(split(whole_ref[...], 3), axis=0)
+    squares = fold(lax.dot_general(factor, factor, NT, preferred_element_type=jnp.float32))
+    gram = (squares[:, :RANK] + squares[:, RANK : 2 * RANK]) + squares[:, 2 * RANK :]
+    share_ref[:, :128] = jnp.concatenate([gram, jnp.zeros((RANK, 128 - RANK), jnp.float32)], axis=1)
     position = lax.axis_index("replica")
     neighbour = position + 1 - 2 * lax.rem(position, 2)
     start = lax.rem(neighbour, 8) * STATE
     share_ref[:, 128:] = whole_ref[:, pl.ds(pl.multiple_of(start, STATE), STATE)]
 
 
-def right_factor(own, other, error, change):
-    rows, columns = error.shape
+def make_share(own, other):
     half = own.shape[1]
-    cost = pl.CostEstimate(
-        flops=12 * RANK * half * columns, bytes_accessed=4 * half * columns, transcendentals=0
-    )
-    projected, gram = pl.pallas_call(
-        first_kernel,
-        in_specs=[VMEM] * 3,
+    return pl.pallas_call(
+        share_kernel,
+        in_specs=[VMEM] * 2,
         out_specs=[VMEM] * 2,
         out_shape=[
-            pltpu.VMEM((RANK, columns), jnp.float32),
-            pltpu.VMEM((RANK, 128), jnp.float32),
+            pltpu.VMEM((RANK, 2 * half), jnp.float32),
+            pltpu.VMEM((RANK, 128 + STATE), jnp.float32),
         ],
         compiler_params=params(8),
-        cost_estimate=cost,
-        name="right_first",
-    )(own, error, change)
-    return pl.pallas_call(
-        second_kernel,
-        in_specs=[VMEM] * 6,
-        out_specs=[VMEM] * 3,
-        out_shape=[
-            pltpu.VMEM((RANK, columns), jnp.float32),
-            pltpu.VMEM((RANK, rows), jnp.float32),
-            pltpu.VMEM((RANK, 128 + STATE), jnp.float32),
-        ],
-        compiler_params=params(8),
-        cost_estimate=cost,
-        name="right_second",
-    )(own, other, error, change, projected, gram)
+        cost_estimate=pl.CostEstimate(
+            flops=36 * RANK * RANK * half, bytes_accessed=24 * RANK * half, transcendentals=0
+        ),
+        name="share",
+    )(own, other)
 
 
 def basis_kernel(whole_ref, mine_ref, theirs_ref, inverse_ref, basis_ref):
@@ -358,7 +364,8 @@
     own = sum_four(own, "y", "x", (1, 3, 2), by_role=True)
     other = swap(own, ("c", 1))
 
-    projected, whole, mine = right_factor(own, other, error, change)
+    projected = right_factor(own, other, error, change)
+    whole, mine = make_share(own, other)
     theirs = swap(mine, ("z", 1))
     summed = sum_four(projected, "y", "z", (3, 1, 2))
     summed, theirs = lax.optimization_barrier((summed, theirs))

time: 63.5 us -> 63.2 us (level)
    pallas_call x2 -> x3, Pallas kernels: 2.88 us -> 2.99 us  [the longest x2 2.63 us: right_factor(): pl.pallas_call(kernel, in_specs=[VMEM] * (3 + len(more)), out_specs=VMEM,...]
where the time goes in v3:
time: 63.2 us; the launch traced here: 63.1 us
  waiting for transfers between devices  21.9 us (35%)
  starting transfers between devices  21.7 us (34%)
  Pallas kernels  18.4 us (29%)
  between operations  0.9 us (1%)
    ppermute x16, waiting for transfers between devices, swap(): return lax.ppermute(value, BOTH, pairs_of((even, odd or even), by_role))  21.9 us
    ppermute x16, starting transfers between devices, swap(): return lax.ppermute(value, BOTH, pairs_of((even, odd or even), by_role))  21.7 us
    pallas_call x1, Pallas kernels, left_factor(): pl.pallas_call(left_kernel, in_specs=[HBM, HBM, HBM], out_specs=[VMEM] *...  5.89 us
    pallas_call x1, Pallas kernels, apply_factors(): pl.pallas_call(lambda *refs: apply_kernel(count, *refs), in_specs=[VMEM]...  5.22 us
    pallas_call x1, Pallas kernels, make_basis(): pl.pallas_call(basis_kernel, in_specs=[VMEM] * 3, out_specs=[VMEM, VMEM],...  3.13 us
    pallas_call x2, Pallas kernels, right_factor(): pl.pallas_call(kernel, in_specs=[VMEM] * (3 + len(more)), out_specs=VMEM,...  2.63 us
  transfers between devices with their start and end apart: 16, of which 11 were waited for; matrix products, arithmetic and copies ran while one was open for 0% of the time, Pallas kernels for 9%

profile of v3, /device:TPU:0, one launch (start us, length us, event | category | flops | bytes accessed | tf_op | source)
XLA Modules:
  0.0 63.1 jit_solution(10446935196052023529)
XLA Ops:
  0.6 5.9 %left_factor.1 = (f32[32,1024]{1,0:T(8,128)S(1)}, f32[32,512]{1,0:T(8,128)S(1)}, bf16[1792,128]{1,0:T(8,128)(2,1)S(1)}, bf16[2048,1792]{1,0:T(8,128)(2,1)S(1)}, bf16[2048,1792]{1,0:T(8,128)(2,1)S(1)}) custom-call(f32[32,1792]{1,0:T(8,128)} %q_hbm.1, bf16[2048,1792]{1,0:T(8,128)(2,1)} %error_hbm.1, bf16[2048,1792]{1,0:T(8,128)(2,1)} %change_hbm.1), custom_call_target="tpu_custom_call" | custom-call | flops 1409286144 | bytes 14680064 | tf_op jit(solution)/shard_map/left_factor/pallas_call | solution.py:133
  6.6 1.2 %left_rest.1 = f32[32,1024]{1,0:T(8,128)S(1)} custom-call(bf16[1792,128]{1,0:T(8,128)(2,1)S(1)} %get-tuple-element.15.factor_ref, bf16[2048,1792]{1,0:T(8,128)(2,1)S(1)} %get-tuple-element.16.error_ref.refs_3_, bf16[2048,1792]{1,0:T(8,128)(2,1)S(1)} %get-tuple-element.17.change_ref.refs_4_, f32[32,512]{1,0:T(8,128)S(1)} %get-tuple-element.18.keep_ref), custom_call_target="tpu_custom_call" | custom-call | flops 352321536 | bytes 3670016 | tf_op jit(solution)/shard_map/left_rest/pallas_call | solution.py:155
  8.0 2.9 %collective-permute-start.3 = (f32[32,1024]{1,0:T(8,128)S(1)}, f32[32,1024]{1,0:T(8,128)S(1)}, u32[]{:S(2)}, u32[]{:S(2)}) collective-permute-start(f32[32,1024]{1,0:T(8,128)S(1)} %add.42), channel_id=1, source_target_pairs={{0,7},{1,96},{2,5},{3,98},{4,101},{5,2},{6,103},{7,0},{8,15},{9,10... | collective-permute-start | bytes 393224 | tf_op jit(solution)/shard_map/ppermute | solution.py:40
  11.9 2.9 %collective-permute-done.3 = f32[32,1024]{1,0:T(8,128)S(1)} collective-permute-done((f32[32,1024]{1,0:T(8,128)S(1)}, f32[32,1024]{1,0:T(8,128)S(1)}, u32[]{:S(2)}, u32[]{:S(2)}) %collective-permute-start.3) | collective-permute-done | bytes 131104 | tf_op jit(solution)/shard_map/ppermute | solution.py:40
  14.8 2.0 %collective-permute-done.2 = f32[32,1024]{1,0:T(8,128)S(1)} collective-permute-done((f32[32,1024]{1,0:T(8,128)S(1)}, f32[32,1024]{1,0:T(8,128)S(1)}, u32[]{:S(2)}, u32[]{:S(2)}) %collective-permute-start.2) | collective-permute-done | bytes 131104 | tf_op jit(solution)/shard_map/ppermute | solution.py:40
  16.8 4.0 %collective-permute-start.4 = (f32[32,1024]{1,0:T(8,128)S(1)}, f32[32,1024]{1,0:T(8,128)S(1)}, u32[]{:S(2)}, u32[]{:S(2)}) collective-permute-start(f32[32,1024]{1,0:T(8,128)S(1)} %add_add_fusion.3), channel_id=1, source_target_pairs={{0,16},{1,17},{2,18},{3,19},{4,20},{5,21},{6,22},{7,23},{8,24},{9,... | collective-permute-start | bytes 393224 | tf_op jit(solution)/shard_map/ppermute | solution.py:40
  20.7 4.1 %collective-permute-done.4 = f32[32,1024]{1,0:T(8,128)S(1)} collective-permute-done((f32[32,1024]{1,0:T(8,128)S(1)}, f32[32,1024]{1,0:T(8,128)S(1)}, u32[]{:S(2)}, u32[]{:S(2)}) %collective-permute-start.4) | collective-permute-done | bytes 131104 | tf_op jit(solution)/shard_map/ppermute | solution.py:40
  24.8 2.5 %collective-permute-start.7 = (f32[32,1024]{1,0:T(8,128)S(1)}, f32[32,1024]{1,0:T(8,128)S(1)}, u32[]{:S(2)}, u32[]{:S(2)}) collective-permute-start(f32[32,1024]{1,0:T(8,128)S(1)} %add.46), channel_id=1, source_target_pairs={{0,97},{1,6},{2,99},{3,4},{4,3},{5,100},{6,1},{7,102},{8,105},{9,1... | collective-permute-start | bytes 393224 | tf_op jit(solution)/shard_map/ppermute | solution.py:40
  27.6 1.1 %collective-permute-start.5 = (f32[32,1024]{1,0:T(8,128)S(1)}, f32[32,1024]{1,0:T(8,128)S(1)}, u32[]{:S(2)}, u32[]{:S(2)}) collective-permute-start(f32[32,1024]{1,0:T(8,128)S(1)} %add.46), channel_id=1, source_target_pairs={{0,32},{1,3},{2,34},{3,1},{4,6},{5,37},{6,4},{7,39},{8,40},{9,11},... | collective-permute-start | bytes 393224 | tf_op jit(solution)/shard_map/ppermute | solution.py:40
  28.7 2.5 %collective-permute-done.7 = f32[32,1024]{1,0:T(8,128)S(1)} collective-permute-done((f32[32,1024]{1,0:T(8,128)S(1)}, f32[32,1024]{1,0:T(8,128)S(1)}, u32[]{:S(2)}, u32[]{:S(2)}) %collective-permute-start.7) | collective-permute-done | bytes 131104 | tf_op jit(solution)/shard_map/ppermute | solution.py:40
  31.3 2.0 %collective-permute-done.6 = f32[32,1024]{1,0:T(8,128)S(1)} collective-permute-done((f32[32,1024]{1,0:T(8,128)S(1)}, f32[32,1024]{1,0:T(8,128)S(1)}, u32[]{:S(2)}, u32[]{:S(2)}) %collective-permute-start.6) | collective-permute-done | bytes 131104 | tf_op jit(solution)/shard_map/ppermute | solution.py:40
  33.4 1.3 %right_first.1.previous_ref = f32[32,1792]{1,0:T(8,128)S(1)} custom-call(f32[32,1024]{1,0:T(8,128)S(1)} %add_add_fusion.2.own_ref, bf16[2048,1792]{1,0:T(8,128)(2,1)S(1)} %get-tuple-element.16.error_ref.refs_3_, bf16[2048,1792]{1,0:T(8,128)(2,1)S(1)} %get-tuple-element.17.change_ref.refs_4_), custom_call_target="tpu_custom_call" | custom-call | flops 704643072 | bytes 7340032 | tf_op jit(solution)/shard_map/right_first/pallas_call | solution.py:199
  34.7 1.3 %right_second.1 = f32[32,1792]{1,0:T(8,128)S(1)} custom-call(f32[32,1024]{1,0:T(8,128)S(1)} %collective-permute-done.8.other_ref, bf16[2048,1792]{1,0:T(8,128)(2,1)S(1)} %get-tuple-element.16.error_ref.refs_3_, bf16[2048,1792]{1,0:T(8,128)(2,1)S(1)} %get-tuple-element.17.change_ref.refs_4_, f32[32,1792]{1,0:T(8,128)S(1)} %right_first.1.previous_ref), custom_call_target="tpu_custom_call" | custom-call | flops 704643072 | bytes 7340032 | tf_op jit(solution)/shard_map/right_second/pallas_call | solution.py:199
  36.0 2.7 %collective-permute-start.11 = (f32[32,1792]{1,0:T(8,128)S(1)}, f32[32,1792]{1,0:T(8,128)S(1)}, u32[]{:S(2)}, u32[]{:S(2)}) collective-permute-start(f32[32,1792]{1,0:T(8,128)S(1)} %right_second.1), channel_id=1, source_target_pairs={{0,96},{1,25},{2,98},{3,27},{4,100},{5,29},{6,102},{7,31},{8,104},... | collective-permute-start | bytes 688136 | tf_op jit(solution)/shard_map/ppermute | solution.py:40
  39.1 1.1 %collective-permute-start.9 = (f32[32,1792]{1,0:T(8,128)S(1)}, f32[32,1792]{1,0:T(8,128)S(1)}, u32[]{:S(2)}, u32[]{:S(2)}) collective-permute-start(f32[32,1792]{1,0:T(8,128)S(1)} %right_second.1), channel_id=1, source_target_pairs={{0,32},{1,9},{2,34},{3,11},{4,36},{5,13},{6,38},{7,15},{8,40},{9,1... | collective-permute-start | bytes 688136 | tf_op jit(solution)/shard_map/ppermute | solution.py:40
  40.5 1.3 %collective-permute-start.12 = (f32[32,384]{1,0:T(8,128)S(1)}, f32[32,384]{1,0:T(8,128)S(1)}, u32[]{:S(2)}, u32[]{:S(2)}) collective-permute-start(f32[32,384]{1,0:T(8,128)S(1)} %get-tuple-element.20.mine_ref), channel_id=1, source_target_pairs={{0,8},{1,9},{2,10},{3,11},{4,12},{5,13},{6,14},{7,15},{8,0},{9,1},... | collective-permute-start | bytes 147464 | tf_op jit(solution)/shard_map/ppermute | solution.py:40
  41.8 2.9 %collective-permute-done.11 = f32[32,1792]{1,0:T(8,128)S(1)} collective-permute-done((f32[32,1792]{1,0:T(8,128)S(1)}, f32[32,1792]{1,0:T(8,128)S(1)}, u32[]{:S(2)}, u32[]{:S(2)}) %collective-permute-start.11) | collective-permute-done | bytes 229408 | tf_op jit(solution)/shard_map/ppermute | solution.py:40
  44.7 1.5 %collective-permute-done.10 = f32[32,1792]{1,0:T(8,128)S(1)} collective-permute-done((f32[32,1792]{1,0:T(8,128)S(1)}, f32[32,1792]{1,0:T(8,128)S(1)}, u32[]{:S(2)}, u32[]{:S(2)}) %collective-permute-start.10) | collective-permute-done | bytes 229408 | tf_op jit(solution)/shard_map/ppermute | solution.py:40
  46.7 3.4 %collective-permute-start.15 = (f32[32,1792]{1,0:T(8,128)S(1)}, f32[32,1792]{1,0:T(8,128)S(1)}, u32[]{:S(2)}, u32[]{:S(2)}) collective-permute-start(f32[32,1792]{1,0:T(8,128)S(1)} %add_add_fusion.1), channel_id=1, source_target_pairs={{0,24},{1,97},{2,26},{3,99},{4,28},{5,101},{6,30},{7,103},{8,16},{... | collective-permute-start | bytes 688136 | tf_op jit(solution)/shard_map/ppermute | solution.py:40
  50.1 0.9 %collective-permute-start.13 = (f32[32,1792]{1,0:T(8,128)S(1)}, f32[32,1792]{1,0:T(8,128)S(1)}, u32[]{:S(2)}, u32[]{:S(2)}) collective-permute-start(f32[32,1792]{1,0:T(8,128)S(1)} %add_add_fusion.1), channel_id=1, source_target_pairs={{0,8},{1,33},{2,10},{3,35},{4,12},{5,37},{6,14},{7,39},{8,0},{9,41... | collective-permute-start | bytes 688136 | tf_op jit(solution)/shard_map/ppermute | solution.py:40
  51.1 3.1 %basis.1 = (f32[32,128]{1,0:T(8,128)S(1)}, bf16[2304,128]{1,0:T(8,128)(2,1)S(1)}) custom-call(f32[32,2048]{1,0:T(8,128)S(1)} %get-tuple-element.22.whole_ref, f32[32,384]{1,0:T(8,128)S(1)} %get-tuple-element.20.mine_ref, f32[32,384]{1,0:T(8,128)S(1)} %collective-permute-done.12.theirs_ref), custom_call_target="tpu_custom_call" | custom-call | flops 50331648 | bytes 1048576 | tf_op jit(solution)/shard_map/basis/pallas_call | solution.py:274
  54.2 1.9 %collective-permute-done.15 = f32[32,1792]{1,0:T(8,128)S(1)} collective-permute-done((f32[32,1792]{1,0:T(8,128)S(1)}, f32[32,1792]{1,0:T(8,128)S(1)}, u32[]{:S(2)}, u32[]{:S(2)}) %collective-permute-start.15) | collective-permute-done | bytes 229408 | tf_op jit(solution)/shard_map/ppermute | solution.py:40
  56.1 1.5 %collective-permute-done.14 = f32[32,1792]{1,0:T(8,128)S(1)} collective-permute-done((f32[32,1792]{1,0:T(8,128)S(1)}, f32[32,1792]{1,0:T(8,128)S(1)}, u32[]{:S(2)}, u32[]{:S(2)}) %collective-permute-start.14) | collective-permute-done | bytes 229408 | tf_op jit(solution)/shard_map/ppermute | solution.py:40
  57.7 5.2 %apply.1 = (bf16[256,1792]{1,0:T(8,128)(2,1)}, f32[256,1792]{1,0:T(8,128)}, bf16[2048,1792]{1,0:T(8,128)(2,1)}, f32[32,1792]{1,0:T(8,128)}) custom-call(f32[32,1792]{1,0:T(8,128)S(1)} %add_add_fusion.refs_0_, f32[32,128]{1,0:T(8,128)S(1)} %get-tuple-element.24.refs_1_, bf16[2304,128]{1,0:T(8,128)(2,1)S(1)} %get-tuple-element.25.refs_2_, ...), custom_call_target="tpu_custom_call" | custom-call | flops 939524096 | bytes 22020096 | tf_op jit(solution)/shard_map/apply/pallas_call | solution.py:333
  (23 shorter events, 3.0 us)
Async XLA Ops:
  6.5 1.4 %collective-permute-start = (f32[32,1024]{1,0:T(8,128)S(1)}, f32[32,1024]{1,0:T(8,128)S(1)}, u32[]{:S(2)}, u32[]{:S(2)}) collective-permute-start(f32[32,1024]{1,0:T(8,128)S(1)} %get-tuple-element.19), channel_id=1, source_target_pairs={{0,1},{1,0},{2,3},{3,2},{4,5},{5,4},{6,7},{7,6},{8,9},{9,8},{10,11... | collective-permute-start | bytes 393224 | tf_op jit(solution)/shard_map/ppermute | solution.py:40
  8.0 6.8 %collective-permute-start.3 = (f32[32,1024]{1,0:T(8,128)S(1)}, f32[32,1024]{1,0:T(8,128)S(1)}, u32[]{:S(2)}, u32[]{:S(2)}) collective-permute-start(f32[32,1024]{1,0:T(8,128)S(1)} %add.42), channel_id=1, source_target_pairs={{0,7},{1,96},{2,5},{3,98},{4,101},{5,2},{6,103},{7,0},{8,15},{9,10... | collective-permute-start | bytes 393224 | tf_op jit(solution)/shard_map/ppermute | solution.py:40
  10.9 5.9 %collective-permute-start.2 = (f32[32,1024]{1,0:T(8,128)S(1)}, f32[32,1024]{1,0:T(8,128)S(1)}, u32[]{:S(2)}, u32[]{:S(2)}) collective-permute-start(f32[32,1024]{1,0:T(8,128)S(1)} %add.42), channel_id=1, source_target_pairs={{0,5},{1,64},{2,7},{3,66},{4,69},{5,0},{6,71},{7,2},{8,13},{9,72},... | collective-permute-start | bytes 393224 | tf_op jit(solution)/shard_map/ppermute | solution.py:40
  11.4 5.3 %collective-permute-start.1 = (f32[32,1024]{1,0:T(8,128)S(1)}, f32[32,1024]{1,0:T(8,128)S(1)}, u32[]{:S(2)}, u32[]{:S(2)}) collective-permute-start(f32[32,1024]{1,0:T(8,128)S(1)} %add.42), channel_id=1, source_target_pairs={{0,2},{1,33},{2,0},{3,35},{4,36},{5,7},{6,38},{7,5},{8,10},{9,41},... | collective-permute-start | bytes 393224 | tf_op jit(solution)/shard_map/ppermute | solution.py:40
  16.8 8.0 %collective-permute-start.4 = (f32[32,1024]{1,0:T(8,128)S(1)}, f32[32,1024]{1,0:T(8,128)S(1)}, u32[]{:S(2)}, u32[]{:S(2)}) collective-permute-start(f32[32,1024]{1,0:T(8,128)S(1)} %add_add_fusion.3), channel_id=1, source_target_pairs={{0,16},{1,17},{2,18},{3,19},{4,20},{5,21},{6,22},{7,23},{8,24},{9,... | collective-permute-start | bytes 393224 | tf_op jit(solution)/shard_map/ppermute | solution.py:40
  24.8 6.4 %collective-permute-start.7 = (f32[32,1024]{1,0:T(8,128)S(1)}, f32[32,1024]{1,0:T(8,128)S(1)}, u32[]{:S(2)}, u32[]{:S(2)}) collective-permute-start(f32[32,1024]{1,0:T(8,128)S(1)} %add.46), channel_id=1, source_target_pairs={{0,97},{1,6},{2,99},{3,4},{4,3},{5,100},{6,1},{7,102},{8,105},{9,1... | collective-permute-start | bytes 393224 | tf_op jit(solution)/shard_map/ppermute | solution.py:40
  27.3 5.9 %collective-permute-start.6 = (f32[32,1024]{1,0:T(8,128)S(1)}, f32[32,1024]{1,0:T(8,128)S(1)}, u32[]{:S(2)}, u32[]{:S(2)}) collective-permute-start(f32[32,1024]{1,0:T(8,128)S(1)} %add.46), channel_id=1, source_target_pairs={{0,65},{1,4},{2,67},{3,6},{4,1},{5,68},{6,3},{7,70},{8,73},{9,12},... | collective-permute-start | bytes 393224 | tf_op jit(solution)/shard_map/ppermute | solution.py:40
  27.6 5.6 %collective-permute-start.5 = (f32[32,1024]{1,0:T(8,128)S(1)}, f32[32,1024]{1,0:T(8,128)S(1)}, u32[]{:S(2)}, u32[]{:S(2)}) collective-permute-start(f32[32,1024]{1,0:T(8,128)S(1)} %add.46), channel_id=1, source_target_pairs={{0,32},{1,3},{2,34},{3,1},{4,6},{5,37},{6,4},{7,39},{8,40},{9,11},... | collective-permute-start | bytes 393224 | tf_op jit(solution)/shard_map/ppermute | solution.py:40
  33.3 1.4 %collective-permute-start.8 = (f32[32,1024]{1,0:T(8,128)S(1)}, f32[32,1024]{1,0:T(8,128)S(1)}, u32[]{:S(2)}, u32[]{:S(2)}) collective-permute-start(f32[32,1024]{1,0:T(8,128)S(1)} %add_add_fusion.2.own_ref), channel_id=1, source_target_pairs={{0,1},{1,0},{2,3},{3,2},{4,5},{5,4},{6,7},{7,6},{8,9},{9,8},{10,11... | collective-permute-start | bytes 393224 | tf_op jit(solution)/shard_map/ppermute | solution.py:40
  34.7 23.1 %copy-start = (f32[256,1792]{1,0:T(8,128)S(1)}, f32[256,1792]{1,0:T(8,128)}, u32[]{:S(2)}) copy-start(f32[256,1792]{1,0:T(8,128)} %refs_5_.1) | copy-start | bytes 5505028
  36.0 8.7 %collective-permute-start.11 = (f32[32,1792]{1,0:T(8,128)S(1)}, f32[32,1792]{1,0:T(8,128)S(1)}, u32[]{:S(2)}, u32[]{:S(2)}) collective-permute-start(f32[32,1792]{1,0:T(8,128)S(1)} %right_second.1), channel_id=1, source_target_pairs={{0,96},{1,25},{2,98},{3,27},{4,100},{5,29},{6,102},{7,31},{8,104},... | collective-permute-start | bytes 688136 | tf_op jit(solution)/shard_map/ppermute | solution.py:40
  38.7 7.5 %collective-permute-start.10 = (f32[32,1792]{1,0:T(8,128)S(1)}, f32[32,1792]{1,0:T(8,128)S(1)}, u32[]{:S(2)}, u32[]{:S(2)}) collective-permute-start(f32[32,1792]{1,0:T(8,128)S(1)} %right_second.1), channel_id=1, source_target_pairs={{0,64},{1,17},{2,66},{3,19},{4,68},{5,21},{6,70},{7,23},{8,72},{9,... | collective-permute-start | bytes 688136 | tf_op jit(solution)/shard_map/ppermute | solution.py:40
  39.1 7.6 %collective-permute-start.9 = (f32[32,1792]{1,0:T(8,128)S(1)}, f32[32,1792]{1,0:T(8,128)S(1)}, u32[]{:S(2)}, u32[]{:S(2)}) collective-permute-start(f32[32,1792]{1,0:T(8,128)S(1)} %right_second.1), channel_id=1, source_target_pairs={{0,32},{1,9},{2,34},{3,11},{4,36},{5,13},{6,38},{7,15},{8,40},{9,1... | collective-permute-start | bytes 688136 | tf_op jit(solution)/shard_map/ppermute | solution.py:40
  40.5 6.2 %collective-permute-start.12 = (f32[32,384]{1,0:T(8,128)S(1)}, f32[32,384]{1,0:T(8,128)S(1)}, u32[]{:S(2)}, u32[]{:S(2)}) collective-permute-start(f32[32,384]{1,0:T(8,128)S(1)} %get-tuple-element.20.mine_ref), channel_id=1, source_target_pairs={{0,8},{1,9},{2,10},{3,11},{4,12},{5,13},{6,14},{7,15},{8,0},{9,1},... | collective-permute-start | bytes 147464 | tf_op jit(solution)/shard_map/ppermute | solution.py:40
  46.7 9.4 %collective-permute-start.15 = (f32[32,1792]{1,0:T(8,128)S(1)}, f32[32,1792]{1,0:T(8,128)S(1)}, u32[]{:S(2)}, u32[]{:S(2)}) collective-permute-start(f32[32,1792]{1,0:T(8,128)S(1)} %add_add_fusion.1), channel_id=1, source_target_pairs={{0,24},{1,97},{2,26},{3,99},{4,28},{5,101},{6,30},{7,103},{8,16},{... | collective-permute-start | bytes 688136 | tf_op jit(solution)/shard_map/ppermute | solution.py:40
  50.1 7.5 %collective-permute-start.14 = (f32[32,1792]{1,0:T(8,128)S(1)}, f32[32,1792]{1,0:T(8,128)S(1)}, u32[]{:S(2)}, u32[]{:S(2)}) collective-permute-start(f32[32,1792]{1,0:T(8,128)S(1)} %add_add_fusion.1), channel_id=1, source_target_pairs={{0,16},{1,65},{2,18},{3,67},{4,20},{5,69},{6,22},{7,71},{8,24},{9,... | collective-permute-start | bytes 688136 | tf_op jit(solution)/shard_map/ppermute | solution.py:40
  50.1 7.5 %collective-permute-start.13 = (f32[32,1792]{1,0:T(8,128)S(1)}, f32[32,1792]{1,0:T(8,128)S(1)}, u32[]{:S(2)}, u32[]{:S(2)}) collective-permute-start(f32[32,1792]{1,0:T(8,128)S(1)} %add_add_fusion.1), channel_id=1, source_target_pairs={{0,8},{1,33},{2,10},{3,35},{4,12},{5,37},{6,14},{7,39},{8,0},{9,41... | collective-permute-start | bytes 688136 | tf_op jit(solution)/shard_map/ppermute | solution.py:40

commit v4 on v3

--- a/solution.py
+++ b/solution.py
@@ -256,7 +256,8 @@
         factor = work[:, j : j + 1] * scale
         work = jnp.where(row > j, work - factor * scaled, jnp.where(row == j, scaled, work))
     inverse = work[:, RANK : 2 * RANK]
-    inverse_ref[...] = jnp.concatenate([inverse, jnp.zeros((RANK, width - RANK), jnp.float32)], axis=1)
+    one, two, three = split(inverse, 3)
+    inverse_ref[...] = jnp.concatenate([one, two, three, one, two, one, *[jnp.zeros_like(one)] * 2], axis=1)
     rows = whole_ref.shape[1]
     position = lax.axis_index("replica")
     start = lax.rem(position, 8) * STATE
@@ -276,7 +277,7 @@
         in_specs=[VMEM] * 3,
         out_specs=[VMEM, VMEM],
         out_shape=[
-            pltpu.VMEM((RANK, 128), jnp.float32),
+            pltpu.VMEM((RANK, 8 * RANK), jnp.bfloat16),
             pltpu.VMEM((rows + STATE, 128), jnp.bfloat16),
         ],
         compiler_params=params(8),
@@ -293,13 +294,9 @@
     momentum_out_ref, update_ref, error_out_ref, sems,
 ):
     rows, columns = error_ref.shape
-    new_q = (
-        jnp.dot(
-            inverse_ref[:, :RANK], summed_ref[...],
-            precision=lax.Precision.HIGHEST, preferred_element_type=jnp.float32,
-        )
-        / count
-    )
+    one, two, three = split(summed_ref[...], 3)
+    stacked = jnp.concatenate([one, one, one, two, two, three], axis=0)
+    new_q = jnp.dot(inverse_ref[:, : 6 * RANK], stacked, preferred_element_type=jnp.float32) / count
     q_ref[...] = new_q
     top, low = split(new_q, 2)
     factor = jnp.concatenate([top, top, low, low], axis=0)

time: 63.2 us -> 63.2 us (level)
  no operation moved by 1% of the time
where the time goes in v4:
time: 63.2 us; the launch traced here: 63 us
  waiting for transfers between devices  21.9 us (35%)
  starting transfers between devices  21.7 us (34%)
  Pallas kernels  18.3 us (29%)
  between operations  0.9 us (1%)
    ppermute x16, waiting for transfers between devices, swap(): return lax.ppermute(value, BOTH, pairs_of((even, odd or even), by_role))  21.9 us
    ppermute x16, starting transfers between devices, swap(): return lax.ppermute(value, BOTH, pairs_of((even, odd or even), by_role))  21.7 us
    pallas_call x1, Pallas kernels, left_factor(): pl.pallas_call(left_kernel, in_specs=[HBM, HBM, HBM], out_specs=[VMEM] *...  5.89 us
    pallas_call x1, Pallas kernels, apply_factors(): pl.pallas_call(lambda *refs: apply_kernel(count, *refs), in_specs=[VMEM]...  5.15 us
    pallas_call x1, Pallas kernels, make_basis(): pl.pallas_call(basis_kernel, in_specs=[VMEM] * 3, out_specs=[VMEM, VMEM],...  3.13 us
    pallas_call x2, Pallas kernels, right_factor(): pl.pallas_call(kernel, in_specs=[VMEM] * (3 + len(more)), out_specs=VMEM,...  2.63 us
  transfers between devices with their start and end apart: 16, of which 11 were waited for; matrix products, arithmetic and copies ran while one was open for 0% of the time, Pallas kernels for 9%

profile of v4, /device:TPU:0, one launch (start us, length us, event | category | flops | bytes accessed | tf_op | source)
XLA Modules:
  0.0 63.0 jit_solution(7229758549783805227)
XLA Ops:
  0.6 5.9 %left_factor.1 = (f32[32,1024]{1,0:T(8,128)S(1)}, f32[32,512]{1,0:T(8,128)S(1)}, bf16[1792,128]{1,0:T(8,128)(2,1)S(1)}, bf16[2048,1792]{1,0:T(8,128)(2,1)S(1)}, bf16[2048,1792]{1,0:T(8,128)(2,1)S(1)}) custom-call(f32[32,1792]{1,0:T(8,128)} %q_hbm.1, bf16[2048,1792]{1,0:T(8,128)(2,1)} %error_hbm.1, bf16[2048,1792]{1,0:T(8,128)(2,1)} %change_hbm.1), custom_call_target="tpu_custom_call" | custom-call | flops 1409286144 | bytes 14680064 | tf_op jit(solution)/shard_map/left_factor/pallas_call | solution.py:133
  6.6 1.2 %left_rest.1 = f32[32,1024]{1,0:T(8,128)S(1)} custom-call(bf16[1792,128]{1,0:T(8,128)(2,1)S(1)} %get-tuple-element.15.factor_ref, bf16[2048,1792]{1,0:T(8,128)(2,1)S(1)} %get-tuple-element.16.error_ref.refs_3_, bf16[2048,1792]{1,0:T(8,128)(2,1)S(1)} %get-tuple-element.17.change_ref.refs_4_, f32[32,512]{1,0:T(8,128)S(1)} %get-tuple-element.18.keep_ref), custom_call_target="tpu_custom_call" | custom-call | flops 352321536 | bytes 3670016 | tf_op jit(solution)/shard_map/left_rest/pallas_call | solution.py:155
  8.0 2.9 %collective-permute-start.3 = (f32[32,1024]{1,0:T(8,128)S(1)}, f32[32,1024]{1,0:T(8,128)S(1)}, u32[]{:S(2)}, u32[]{:S(2)}) collective-permute-start(f32[32,1024]{1,0:T(8,128)S(1)} %add.42), channel_id=1, source_target_pairs={{0,7},{1,96},{2,5},{3,98},{4,101},{5,2},{6,103},{7,0},{8,15},{9,10... | collective-permute-start | bytes 393224 | tf_op jit(solution)/shard_map/ppermute | solution.py:40
  11.9 2.9 %collective-permute-done.3 = f32[32,1024]{1,0:T(8,128)S(1)} collective-permute-done((f32[32,1024]{1,0:T(8,128)S(1)}, f32[32,1024]{1,0:T(8,128)S(1)}, u32[]{:S(2)}, u32[]{:S(2)}) %collective-permute-start.3) | collective-permute-done | bytes 131104 | tf_op jit(solution)/shard_map/ppermute | solution.py:40
  14.8 2.0 %collective-permute-done.2 = f32[32,1024]{1,0:T(8,128)S(1)} collective-permute-done((f32[32,1024]{1,0:T(8,128)S(1)}, f32[32,1024]{1,0:T(8,128)S(1)}, u32[]{:S(2)}, u32[]{:S(2)}) %collective-permute-start.2) | collective-permute-done | bytes 131104 | tf_op jit(solution)/shard_map/ppermute | solution.py:40
  16.8 4.0 %collective-permute-start.4 = (f32[32,1024]{1,0:T(8,128)S(1)}, f32[32,1024]{1,0:T(8,128)S(1)}, u32[]{:S(2)}, u32[]{:S(2)}) collective-permute-start(f32[32,1024]{1,0:T(8,128)S(1)} %add_add_fusion.3), channel_id=1, source_target_pairs={{0,16},{1,17},{2,18},{3,19},{4,20},{5,21},{6,22},{7,23},{8,24},{9,... | collective-permute-start | bytes 393224 | tf_op jit(solution)/shard_map/ppermute | solution.py:40
  20.7 4.1 %collective-permute-done.4 = f32[32,1024]{1,0:T(8,128)S(1)} collective-permute-done((f32[32,1024]{1,0:T(8,128)S(1)}, f32[32,1024]{1,0:T(8,128)S(1)}, u32[]{:S(2)}, u32[]{:S(2)}) %collective-permute-start.4) | collective-permute-done | bytes 131104 | tf_op jit(solution)/shard_map/ppermute | solution.py:40
  24.8 2.5 %collective-permute-start.7 = (f32[32,1024]{1,0:T(8,128)S(1)}, f32[32,1024]{1,0:T(8,128)S(1)}, u32[]{:S(2)}, u32[]{:S(2)}) collective-permute-start(f32[32,1024]{1,0:T(8,128)S(1)} %add.46), channel_id=1, source_target_pairs={{0,97},{1,6},{2,99},{3,4},{4,3},{5,100},{6,1},{7,102},{8,105},{9,1... | collective-permute-start | bytes 393224 | tf_op jit(solution)/shard_map/ppermute | solution.py:40
  27.6 1.1 %collective-permute-start.5 = (f32[32,1024]{1,0:T(8,128)S(1)}, f32[32,1024]{1,0:T(8,128)S(1)}, u32[]{:S(2)}, u32[]{:S(2)}) collective-permute-start(f32[32,1024]{1,0:T(8,128)S(1)} %add.46), channel_id=1, source_target_pairs={{0,32},{1,3},{2,34},{3,1},{4,6},{5,37},{6,4},{7,39},{8,40},{9,11},... | collective-permute-start | bytes 393224 | tf_op jit(solution)/shard_map/ppermute | solution.py:40
  28.7 2.5 %collective-permute-done.7 = f32[32,1024]{1,0:T(8,128)S(1)} collective-permute-done((f32[32,1024]{1,0:T(8,128)S(1)}, f32[32,1024]{1,0:T(8,128)S(1)}, u32[]{:S(2)}, u32[]{:S(2)}) %collective-permute-start.7) | collective-permute-done | bytes 131104 | tf_op jit(solution)/shard_map/ppermute | solution.py:40
  31.3 2.0 %collective-permute-done.6 = f32[32,1024]{1,0:T(8,128)S(1)} collective-permute-done((f32[32,1024]{1,0:T(8,128)S(1)}, f32[32,1024]{1,0:T(8,128)S(1)}, u32[]{:S(2)}, u32[]{:S(2)}) %collective-permute-start.6) | collective-permute-done | bytes 131104 | tf_op jit(solution)/shard_map/ppermute | solution.py:40
  33.4 1.3 %right_first.1.previous_ref = f32[32,1792]{1,0:T(8,128)S(1)} custom-call(f32[32,1024]{1,0:T(8,128)S(1)} %add_add_fusion.2.own_ref, bf16[2048,1792]{1,0:T(8,128)(2,1)S(1)} %get-tuple-element.16.error_ref.refs_3_, bf16[2048,1792]{1,0:T(8,128)(2,1)S(1)} %get-tuple-element.17.change_ref.refs_4_), custom_call_target="tpu_custom_call" | custom-call | flops 704643072 | bytes 7340032 | tf_op jit(solution)/shard_map/right_first/pallas_call | solution.py:199
  34.7 1.3 %right_second.1 = f32[32,1792]{1,0:T(8,128)S(1)} custom-call(f32[32,1024]{1,0:T(8,128)S(1)} %collective-permute-done.8.other_ref, bf16[2048,1792]{1,0:T(8,128)(2,1)S(1)} %get-tuple-element.16.error_ref.refs_3_, bf16[2048,1792]{1,0:T(8,128)(2,1)S(1)} %get-tuple-element.17.change_ref.refs_4_, f32[32,1792]{1,0:T(8,128)S(1)} %right_first.1.previous_ref), custom_call_target="tpu_custom_call" | custom-call | flops 704643072 | bytes 7340032 | tf_op jit(solution)/shard_map/right_second/pallas_call | solution.py:199
  36.0 2.7 %collective-permute-start.11 = (f32[32,1792]{1,0:T(8,128)S(1)}, f32[32,1792]{1,0:T(8,128)S(1)}, u32[]{:S(2)}, u32[]{:S(2)}) collective-permute-start(f32[32,1792]{1,0:T(8,128)S(1)} %right_second.1), channel_id=1, source_target_pairs={{0,96},{1,25},{2,98},{3,27},{4,100},{5,29},{6,102},{7,31},{8,104},... | collective-permute-start | bytes 688136 | tf_op jit(solution)/shard_map/ppermute | solution.py:40
  39.1 1.1 %collective-permute-start.9 = (f32[32,1792]{1,0:T(8,128)S(1)}, f32[32,1792]{1,0:T(8,128)S(1)}, u32[]{:S(2)}, u32[]{:S(2)}) collective-permute-start(f32[32,1792]{1,0:T(8,128)S(1)} %right_second.1), channel_id=1, source_target_pairs={{0,32},{1,9},{2,34},{3,11},{4,36},{5,13},{6,38},{7,15},{8,40},{9,1... | collective-permute-start | bytes 688136 | tf_op jit(solution)/shard_map/ppermute | solution.py:40
  40.5 1.3 %collective-permute-start.12 = (f32[32,384]{1,0:T(8,128)S(1)}, f32[32,384]{1,0:T(8,128)S(1)}, u32[]{:S(2)}, u32[]{:S(2)}) collective-permute-start(f32[32,384]{1,0:T(8,128)S(1)} %get-tuple-element.20.mine_ref), channel_id=1, source_target_pairs={{0,8},{1,9},{2,10},{3,11},{4,12},{5,13},{6,14},{7,15},{8,0},{9,1},... | collective-permute-start | bytes 147464 | tf_op jit(solution)/shard_map/ppermute | solution.py:40
  41.8 2.9 %collective-permute-done.11 = f32[32,1792]{1,0:T(8,128)S(1)} collective-permute-done((f32[32,1792]{1,0:T(8,128)S(1)}, f32[32,1792]{1,0:T(8,128)S(1)}, u32[]{:S(2)}, u32[]{:S(2)}) %collective-permute-start.11) | collective-permute-done | bytes 229408 | tf_op jit(solution)/shard_map/ppermute | solution.py:40
  44.7 1.5 %collective-permute-done.10 = f32[32,1792]{1,0:T(8,128)S(1)} collective-permute-done((f32[32,1792]{1,0:T(8,128)S(1)}, f32[32,1792]{1,0:T(8,128)S(1)}, u32[]{:S(2)}, u32[]{:S(2)}) %collective-permute-start.10) | collective-permute-done | bytes 229408 | tf_op jit(solution)/shard_map/ppermute | solution.py:40
  46.7 3.4 %collective-permute-start.15 = (f32[32,1792]{1,0:T(8,128)S(1)}, f32[32,1792]{1,0:T(8,128)S(1)}, u32[]{:S(2)}, u32[]{:S(2)}) collective-permute-start(f32[32,1792]{1,0:T(8,128)S(1)} %add_add_fusion.1), channel_id=1, source_target_pairs={{0,24},{1,97},{2,26},{3,99},{4,28},{5,101},{6,30},{7,103},{8,16},{... | collective-permute-start | bytes 688136 | tf_op jit(solution)/shard_map/ppermute | solution.py:40
  50.1 0.9 %collective-permute-start.13 = (f32[32,1792]{1,0:T(8,128)S(1)}, f32[32,1792]{1,0:T(8,128)S(1)}, u32[]{:S(2)}, u32[]{:S(2)}) collective-permute-start(f32[32,1792]{1,0:T(8,128)S(1)} %add_add_fusion.1), channel_id=1, source_target_pairs={{0,8},{1,33},{2,10},{3,35},{4,12},{5,37},{6,14},{7,39},{8,0},{9,41... | collective-permute-start | bytes 688136 | tf_op jit(solution)/shard_map/ppermute | solution.py:40
  51.1 3.1 %basis.1 = (bf16[32,256]{1,0:T(8,128)(2,1)S(1)}, bf16[2304,128]{1,0:T(8,128)(2,1)S(1)}) custom-call(f32[32,2048]{1,0:T(8,128)S(1)} %get-tuple-element.22.whole_ref, f32[32,384]{1,0:T(8,128)S(1)} %get-tuple-element.20.mine_ref, f32[32,384]{1,0:T(8,128)S(1)} %collective-permute-done.12.theirs_ref), custom_call_target="tpu_custom_call" | custom-call | flops 50331648 | bytes 1048576 | tf_op jit(solution)/shard_map/basis/pallas_call | solution.py:275
  54.2 1.9 %collective-permute-done.15 = f32[32,1792]{1,0:T(8,128)S(1)} collective-permute-done((f32[32,1792]{1,0:T(8,128)S(1)}, f32[32,1792]{1,0:T(8,128)S(1)}, u32[]{:S(2)}, u32[]{:S(2)}) %collective-permute-start.15) | collective-permute-done | bytes 229408 | tf_op jit(solution)/shard_map/ppermute | solution.py:40
  56.1 1.5 %collective-permute-done.14 = f32[32,1792]{1,0:T(8,128)S(1)} collective-permute-done((f32[32,1792]{1,0:T(8,128)S(1)}, f32[32,1792]{1,0:T(8,128)S(1)}, u32[]{:S(2)}, u32[]{:S(2)}) %collective-permute-start.14) | collective-permute-done | bytes 229408 | tf_op jit(solution)/shard_map/ppermute | solution.py:40
  57.7 5.2 %apply.1 = (bf16[256,1792]{1,0:T(8,128)(2,1)}, f32[256,1792]{1,0:T(8,128)}, bf16[2048,1792]{1,0:T(8,128)(2,1)}, f32[32,1792]{1,0:T(8,128)}) custom-call(f32[32,1792]{1,0:T(8,128)S(1)} %add_add_fusion.refs_0_, bf16[32,256]{1,0:T(8,128)(2,1)S(1)} %get-tuple-element.24.refs_1_, bf16[2304,128]{1,0:T(8,128)(2,1)S(1)} %get-tuple-element.25.refs_2_, ...), custom_call_target="tpu_custom_call" | custom-call | flops 939524096 | bytes 22020096 | tf_op jit(solution)/shard_map/apply/pallas_call | solution.py:330
  (23 shorter events, 3.0 us)
Async XLA Ops:
  6.5 1.4 %collective-permute-start = (f32[32,1024]{1,0:T(8,128)S(1)}, f32[32,1024]{1,0:T(8,128)S(1)}, u32[]{:S(2)}, u32[]{:S(2)}) collective-permute-start(f32[32,1024]{1,0:T(8,128)S(1)} %get-tuple-element.19), channel_id=1, source_target_pairs={{0,1},{1,0},{2,3},{3,2},{4,5},{5,4},{6,7},{7,6},{8,9},{9,8},{10,11... | collective-permute-start | bytes 393224 | tf_op jit(solution)/shard_map/ppermute | solution.py:40
  8.0 6.8 %collective-permute-start.3 = (f32[32,1024]{1,0:T(8,128)S(1)}, f32[32,1024]{1,0:T(8,128)S(1)}, u32[]{:S(2)}, u32[]{:S(2)}) collective-permute-start(f32[32,1024]{1,0:T(8,128)S(1)} %add.42), channel_id=1, source_target_pairs={{0,7},{1,96},{2,5},{3,98},{4,101},{5,2},{6,103},{7,0},{8,15},{9,10... | collective-permute-start | bytes 393224 | tf_op jit(solution)/shard_map/ppermute | solution.py:40
  10.9 5.9 %collective-permute-start.2 = (f32[32,1024]{1,0:T(8,128)S(1)}, f32[32,1024]{1,0:T(8,128)S(1)}, u32[]{:S(2)}, u32[]{:S(2)}) collective-permute-start(f32[32,1024]{1,0:T(8,128)S(1)} %add.42), channel_id=1, source_target_pairs={{0,5},{1,64},{2,7},{3,66},{4,69},{5,0},{6,71},{7,2},{8,13},{9,72},... | collective-permute-start | bytes 393224 | tf_op jit(solution)/shard_map/ppermute | solution.py:40
  11.4 5.3 %collective-permute-start.1 = (f32[32,1024]{1,0:T(8,128)S(1)}, f32[32,1024]{1,0:T(8,128)S(1)}, u32[]{:S(2)}, u32[]{:S(2)}) collective-permute-start(f32[32,1024]{1,0:T(8,128)S(1)} %add.42), channel_id=1, source_target_pairs={{0,2},{1,33},{2,0},{3,35},{4,36},{5,7},{6,38},{7,5},{8,10},{9,41},... | collective-permute-start | bytes 393224 | tf_op jit(solution)/shard_map/ppermute | solution.py:40
  16.8 8.0 %collective-permute-start.4 = (f32[32,1024]{1,0:T(8,128)S(1)}, f32[32,1024]{1,0:T(8,128)S(1)}, u32[]{:S(2)}, u32[]{:S(2)}) collective-permute-start(f32[32,1024]{1,0:T(8,128)S(1)} %add_add_fusion.3), channel_id=1, source_target_pairs={{0,16},{1,17},{2,18},{3,19},{4,20},{5,21},{6,22},{7,23},{8,24},{9,... | collective-permute-start | bytes 393224 | tf_op jit(solution)/shard_map/ppermute | solution.py:40
  24.8 6.4 %collective-permute-start.7 = (f32[32,1024]{1,0:T(8,128)S(1)}, f32[32,1024]{1,0:T(8,128)S(1)}, u32[]{:S(2)}, u32[]{:S(2)}) collective-permute-start(f32[32,1024]{1,0:T(8,128)S(1)} %add.46), channel_id=1, source_target_pairs={{0,97},{1,6},{2,99},{3,4},{4,3},{5,100},{6,1},{7,102},{8,105},{9,1... | collective-permute-start | bytes 393224 | tf_op jit(solution)/shard_map/ppermute | solution.py:40
  27.3 5.9 %collective-permute-start.6 = (f32[32,1024]{1,0:T(8,128)S(1)}, f32[32,1024]{1,0:T(8,128)S(1)}, u32[]{:S(2)}, u32[]{:S(2)}) collective-permute-start(f32[32,1024]{1,0:T(8,128)S(1)} %add.46), channel_id=1, source_target_pairs={{0,65},{1,4},{2,67},{3,6},{4,1},{5,68},{6,3},{7,70},{8,73},{9,12},... | collective-permute-start | bytes 393224 | tf_op jit(solution)/shard_map/ppermute | solution.py:40
  27.6 5.6 %collective-permute-start.5 = (f32[32,1024]{1,0:T(8,128)S(1)}, f32[32,1024]{1,0:T(8,128)S(1)}, u32[]{:S(2)}, u32[]{:S(2)}) collective-permute-start(f32[32,1024]{1,0:T(8,128)S(1)} %add.46), channel_id=1, source_target_pairs={{0,32},{1,3},{2,34},{3,1},{4,6},{5,37},{6,4},{7,39},{8,40},{9,11},... | collective-permute-start | bytes 393224 | tf_op jit(solution)/shard_map/ppermute | solution.py:40
  33.3 1.4 %collective-permute-start.8 = (f32[32,1024]{1,0:T(8,128)S(1)}, f32[32,1024]{1,0:T(8,128)S(1)}, u32[]{:S(2)}, u32[]{:S(2)}) collective-permute-start(f32[32,1024]{1,0:T(8,128)S(1)} %add_add_fusion.2.own_ref), channel_id=1, source_target_pairs={{0,1},{1,0},{2,3},{3,2},{4,5},{5,4},{6,7},{7,6},{8,9},{9,8},{10,11... | collective-permute-start | bytes 393224 | tf_op jit(solution)/shard_map/ppermute | solution.py:40
  34.7 23.1 %copy-start = (f32[256,1792]{1,0:T(8,128)S(1)}, f32[256,1792]{1,0:T(8,128)}, u32[]{:S(2)}) copy-start(f32[256,1792]{1,0:T(8,128)} %refs_5_.1) | copy-start | bytes 5505028
  36.0 8.7 %collective-permute-start.11 = (f32[32,1792]{1,0:T(8,128)S(1)}, f32[32,1792]{1,0:T(8,128)S(1)}, u32[]{:S(2)}, u32[]{:S(2)}) collective-permute-start(f32[32,1792]{1,0:T(8,128)S(1)} %right_second.1), channel_id=1, source_target_pairs={{0,96},{1,25},{2,98},{3,27},{4,100},{5,29},{6,102},{7,31},{8,104},... | collective-permute-start | bytes 688136 | tf_op jit(solution)/shard_map/ppermute | solution.py:40
  38.7 7.5 %collective-permute-start.10 = (f32[32,1792]{1,0:T(8,128)S(1)}, f32[32,1792]{1,0:T(8,128)S(1)}, u32[]{:S(2)}, u32[]{:S(2)}) collective-permute-start(f32[32,1792]{1,0:T(8,128)S(1)} %right_second.1), channel_id=1, source_target_pairs={{0,64},{1,17},{2,66},{3,19},{4,68},{5,21},{6,70},{7,23},{8,72},{9,... | collective-permute-start | bytes 688136 | tf_op jit(solution)/shard_map/ppermute | solution.py:40
  39.1 7.6 %collective-permute-start.9 = (f32[32,1792]{1,0:T(8,128)S(1)}, f32[32,1792]{1,0:T(8,128)S(1)}, u32[]{:S(2)}, u32[]{:S(2)}) collective-permute-start(f32[32,1792]{1,0:T(8,128)S(1)} %right_second.1), channel_id=1, source_target_pairs={{0,32},{1,9},{2,34},{3,11},{4,36},{5,13},{6,38},{7,15},{8,40},{9,1... | collective-permute-start | bytes 688136 | tf_op jit(solution)/shard_map/ppermute | solution.py:40
  40.5 6.2 %collective-permute-start.12 = (f32[32,384]{1,0:T(8,128)S(1)}, f32[32,384]{1,0:T(8,128)S(1)}, u32[]{:S(2)}, u32[]{:S(2)}) collective-permute-start(f32[32,384]{1,0:T(8,128)S(1)} %get-tuple-element.20.mine_ref), channel_id=1, source_target_pairs={{0,8},{1,9},{2,10},{3,11},{4,12},{5,13},{6,14},{7,15},{8,0},{9,1},... | collective-permute-start | bytes 147464 | tf_op jit(solution)/shard_map/ppermute | solution.py:40
  46.7 9.4 %collective-permute-start.15 = (f32[32,1792]{1,0:T(8,128)S(1)}, f32[32,1792]{1,0:T(8,128)S(1)}, u32[]{:S(2)}, u32[]{:S(2)}) collective-permute-start(f32[32,1792]{1,0:T(8,128)S(1)} %add_add_fusion.1), channel_id=1, source_target_pairs={{0,24},{1,97},{2,26},{3,99},{4,28},{5,101},{6,30},{7,103},{8,16},{... | collective-permute-start | bytes 688136 | tf_op jit(solution)/shard_map/ppermute | solution.py:40
  50.1 7.5 %collective-permute-start.14 = (f32[32,1792]{1,0:T(8,128)S(1)}, f32[32,1792]{1,0:T(8,128)S(1)}, u32[]{:S(2)}, u32[]{:S(2)}) collective-permute-start(f32[32,1792]{1,0:T(8,128)S(1)} %add_add_fusion.1), channel_id=1, source_target_pairs={{0,16},{1,65},{2,18},{3,67},{4,20},{5,69},{6,22},{7,71},{8,24},{9,... | collective-permute-start | bytes 688136 | tf_op jit(solution)/shard_map/ppermute | solution.py:40
  50.1 7.5 %collective-permute-start.13 = (f32[32,1792]{1,0:T(8,128)S(1)}, f32[32,1792]{1,0:T(8,128)S(1)}, u32[]{:S(2)}, u32[]{:S(2)}) collective-permute-start(f32[32,1792]{1,0:T(8,128)S(1)} %add_add_fusion.1), channel_id=1, source_target_pairs={{0,8},{1,33},{2,10},{3,35},{4,12},{5,37},{6,14},{7,39},{8,0},{9,41... | collective-permute-start | bytes 688136 | tf_op jit(solution)/shard_map/ppermute | solution.py:40
